TPU v7x, 32 devices: a whole 2x2x4 slice. The times are simulated.
32 devices in a mesh: groups: 2 (over y), space: 4 (over z), batch: 4 (over x, core).
Axes of the slice: x: 2, y: 2, z: 4, core: 2. Of those that a mesh axis runs over, the one named last changes fastest.
Arguments:
- fields: bfloat16 [8, 32, 64, 128], P(('groups', 'batch'), 'space'), parts along dimension 0, may hold values from -36 to 36
- land: int32 [32, 64], P('space'), may hold values 0 or 1
- conv_in: bfloat16 [9, 128, 128], replicated, may hold values from -0.1875 to 0.1875
- conv_out: bfloat16 [9, 128, 128], replicated, may hold values from -0.1875 to 0.1875
- batchnorm_gain: float32 [128], replicated, may hold values from 0.25 to 1.75
- batchnorm_offset: float32 [128], replicated, may hold values from -3 to 3
- target_grad: bfloat16 [8, 32, 64, 128], P(('groups', 'batch'), 'space'), parts along dimension 0, may hold values from -6 to 6
Outputs:
- output: bfloat16 [8, 32, 64, 128], P(('groups', 'batch'), 'space'), parts along dimension 0
- grad_in: float32 [18, 128, 128], P('groups', None, 'batch'), parts along dimension 0
- grad_out: float32 [18, 128, 128], P('groups', None, 'batch'), parts along dimension 0
- gain_gradient: float32 [256], P('groups'), parts along dimension 0
- offset_gradient: float32 [256], P('groups'), parts along dimension 0
There are 2 independent parts, one for each index of `groups`. A program takes and returns all parts, laid end to end along the dimension named above; an argument that names none is the same for every part. Nothing has to cross between parts.
All inputs are finite; a program needn't handle non-finite values. No bound on the sum of `land` on one device may be relied on, other than what follows from the above.
Results may differ from a plain program's by a relative error of at most 0.025.
Values may be sent and summed in bfloat16 or wider, within the bound.
A program may use at most 64 MiB of HBM per device.

v0:
```python
import jax
import jax.numpy as jnp
from jax import lax
from jax.sharding import PartitionSpec as P


def partner(value, axis, distance):
    mask = 2**distance
    pairs = [(source, source ^ mask) for source in range(lax.axis_size(axis))]
    return lax.ppermute(value, axis, pairs)


def extended_2(x, sides, width):
    for axis, dim in sides:
        size, length = (lax.axis_size(axis), x.shape[dim])
        up = [(i, (i + 1) % size) for i in range(size)]
        down = [(j, i) for i, j in up]
        last = lax.slice_in_dim(x, length - width, length, axis=dim)
        initial = lax.slice_in_dim(x, 0, width, axis=dim)
        before = lax.ppermute(last, axis, up)
        after = lax.ppermute(initial, axis, down)
        x = jnp.concatenate([before, x, after], axis=dim)
    return x


def mirror_row(row_part):
    steps_total = lax.axis_size("space").bit_length() - 1
    moved = row_part
    for bit_number in range(steps_total):
        moved = partner(moved, "space", bit_number)
    return jnp.flip(moved, axis=1)


def surround(field):
    ghost = mirror_row(field[:, :, -1, :])
    south = jnp.zeros_like(field[:, :, :1, :])
    extended = jnp.concatenate([south, field, ghost[:, :, None, :]], axis=2)
    return extended_2(extended, (("space", 1),), 1)


def convolve(padded, weights, lon, lat):
    chans = padded.shape[3]
    total = jnp.zeros((padded.shape[0] * lon * lat, weights.shape[2]), jnp.float32)
    for tap in range(9):
        first, second = (tap // 3, tap % 3)
        piece = padded[:, first : first + lon, second : second + lat, :].reshape(-1, chans)
        total = total + jnp.dot(piece, weights[tap], preferred_element_type=jnp.float32)
    return total.reshape(padded.shape[0], lon, lat, weights.shape[2])


def adjoint_conv(padded, weights, lon, lat):
    chans = padded.shape[3]
    ghost_row = padded[:, :, lat + 1, :]
    cleared = padded.at[:, :, lat + 1, :].set(jnp.zeros_like(ghost_row))
    total = jnp.zeros((padded.shape[0] * lon * lat, weights.shape[1]), jnp.float32)
    for tap in range(9):
        first, second = (tap // 3, tap % 3)
        piece = cleared[:, 2 - first : 2 - first + lon, 2 - second : 2 - second + lat, :].reshape(
            -1, chans
        )
        total = total + lax.dot_general(
            piece, weights[tap], (((1,), (1,)), ((), ())), preferred_element_type=jnp.float32
        )
    total = total.reshape(padded.shape[0], lon, lat, weights.shape[1])
    extra = jnp.zeros((padded.shape[0] * lon, weights.shape[1]), jnp.float32)
    for first in range(3):
        piece = ghost_row[:, first : first + lon, :].reshape(-1, chans)
        extra = extra + lax.dot_general(
            piece,
            weights[3 * first + 2],
            (((1,), (1,)), ((), ())),
            preferred_element_type=jnp.float32,
        )
    extra = extra.reshape(padded.shape[0], lon, weights.shape[1])
    return total.at[:, :, lat - 1, :].add(extra)


def tap_grads(padded, grad, lon, lat):
    chans = padded.shape[3]
    flat = grad.reshape(-1, grad.shape[3])
    result = []
    for tap in range(9):
        first, second = (tap // 3, tap % 3)
        piece = padded[:, first : first + lon, second : second + lat, :].reshape(-1, chans)
        result.append(
            lax.dot_general(
                piece, flat, (((0,), (0,)), ((), ())), preferred_element_type=jnp.float32
            )
        )
    return jnp.stack(result, axis=0)


def reduce_weights(partial_grad):
    summed = lax.psum(partial_grad.astype(jnp.bfloat16), "space")
    return lax.psum_scatter(summed, "batch", scatter_dimension=2, tiled=True).astype(jnp.float32)


def gelu_value(value):
    inner = 0.7978845608 * (value + 0.044715 * value * value * value)
    return 0.5 * value * (1.0 + jnp.tanh(inner))


def gelu_slope(value):
    inner = 0.7978845608 * (value + 0.044715 * value * value * value)
    hyper = jnp.tanh(inner)
    return 0.5 * (1.0 + hyper) + 0.5 * value * (1.0 - hyper * hyper) * 0.7978845608 * (
        1.0 + 3.0 * 0.044715 * value * value
    )


def body(fields, land, conv_in, conv_out, batchnorm_gain, batchnorm_offset, target_grad):
    lon, lat = (fields.shape[1], fields.shape[2])
    ocean_mask = land.astype(jnp.float32)[None, :, :, None]
    masked = fields * ocean_mask.astype(jnp.bfloat16)
    padded_in = surround(masked)
    first = convolve(padded_in, conv_in, lon, lat).astype(jnp.bfloat16)
    first_features = first.astype(jnp.float32)
    local_count = jnp.sum(land.astype(jnp.float32)) * fields.shape[0]
    sums, squares, element_count = lax.psum(
        (
            jnp.sum(first_features * ocean_mask, axis=(0, 1, 2)),
            jnp.sum(first_features * first_features * ocean_mask, axis=(0, 1, 2)),
            local_count,
        ),
        ("space", "batch"),
    )
    channel_mean = sums / element_count
    var = squares / element_count - channel_mean * channel_mean
    inverse_deviation = lax.rsqrt(var + 1e-05)
    normalized_input = (first_features - channel_mean) * inverse_deviation
    preactivation = batchnorm_gain * normalized_input + batchnorm_offset
    act = (gelu_value(preactivation) * ocean_mask).astype(jnp.bfloat16)
    padded_act = surround(act)
    output = (convolve(padded_act, conv_out, lon, lat) * ocean_mask).astype(jnp.bfloat16)
    dout = (target_grad.astype(jnp.float32) * ocean_mask * lax.rsqrt(element_count)).astype(
        jnp.bfloat16
    )
    grad_out = reduce_weights(tap_grads(padded_act, dout, lon, lat))
    dact = adjoint_conv(surround(dout), conv_out, lon, lat)
    preactivation_gradient = dact * ocean_mask * gelu_slope(preactivation)
    offset_gradient, gain_gradient = lax.psum(
        (
            jnp.sum(preactivation_gradient, axis=(0, 1, 2)),
            jnp.sum(preactivation_gradient * normalized_input, axis=(0, 1, 2)),
        ),
        ("space", "batch"),
    )
    first_layer_gradient = (
        ocean_mask
        * batchnorm_gain
        * inverse_deviation
        * (
            preactivation_gradient
            - (offset_gradient + normalized_input * gain_gradient) / element_count
        )
    ).astype(jnp.bfloat16)
    grad_in = reduce_weights(tap_grads(padded_in, first_layer_gradient, lon, lat))
    return (output, grad_in, grad_out, gain_gradient, offset_gradient)


def solution(mesh):
    in_specs = (
        P(("groups", "batch"), "space", None, None),
        P("space", None),
        P(),
        P(),
        P(),
        P(),
        P(("groups", "batch"), "space", None, None),
    )
    out_specs = (
        P(("groups", "batch"), "space", None, None),
        P("groups", None, "batch"),
        P("groups", None, "batch"),
        P("groups"),
        P("groups"),
    )
    return jax.shard_map(body, mesh=mesh, in_specs=in_specs, out_specs=out_specs, check_vma=False)
```

profile of v0, /device:TPU:0, one launch (start us, length us, event | category | flops | bytes accessed | tf_op | source)
XLA Modules:
  0.0 216.1 jit_solution(872169914859820042)
XLA Ops:
  7.2 0.7 fusion.202
  7.9 1.0 broadcast_multiply_fusion
  9.0 3.1 %collective-permute-start = (bf16[1,8,128]{2,1,0:T(8,128)(2,1)S(1)}, bf16[1,8,128]{2,1,0:T(8,128)(2,1)S(1)}, u32[]{:S(2)}, u32[]{:S(2)}) collective-permute-start(bf16[1,8,128]{2,1,0:T(8,128)(2,1)S(1)} %bitcast.514), channel_id=1, source_target_pairs={{0,4},{4,0},{8,12},{12,8},{1,5},{5,1},{9,13},{13,9},{2,6},{6,2},{1... | collective-permute-start | bytes 6152 | tf_op jit(solution)/shard_map/ppermute | solution.py:10
  12.1 1.6 collective-permute-done
  13.6 3.0 %collective-permute-start.1 = (bf16[1,8,128]{2,1,0:T(8,128)(2,1)S(1)}, bf16[1,8,128]{2,1,0:T(8,128)(2,1)S(1)}, u32[]{:S(2)}, u32[]{:S(2)}) collective-permute-start(bf16[1,8,128]{2,1,0:T(8,128)(2,1)S(1)} %collective-permute-done), channel_id=1, source_target_pairs={{0,8},{4,12},{8,0},{12,4},{1,9},{5,13},{9,1},{13,5},{2,10},{6,14},... | collective-permute-start | bytes 6152 | tf_op jit(solution)/shard_map/ppermute | solution.py:10
  16.7 0.6 convert_reduce_fusion
  17.4 0.9 collective-permute-done.1
  18.3 4.0 %collective-permute-start.3 = (bf16[1,1,66,128]{3,2,1,0:T(8,128)(2,1)S(1)}, bf16[1,1,66,128]{3,2,1,0:T(8,128)(2,1)S(1)}, u32[]{:S(2)}, u32[]{:S(2)}) collective-permute-start(bf16[1,1,66,128]{3,2,1,0:T(8,128)(2,1)S(1)} %get-tuple-element.94), channel_id=1, source_target_pairs={{4,0},{8,4},{12,8},{0,12},{5,1},{9,5},{13,9},{1,13},{6,2},{10,6},{... | collective-permute-start | bytes 50696 | tf_op jit(solution)/shard_map/ppermute | solution.py:21
  22.4 1.4 collective-permute-done.3
  23.8 4.1 %collective-permute-done.2 = bf16[1,1,66,128]{3,2,1,0:T(8,128)(2,1)S(1)} collective-permute-done((bf16[1,1,66,128]{3,2,1,0:T(8,128)(2,1)S(1)}, bf16[1,1,66,128]{3,2,1,0:T(8,128)(2,1)S(1)}, u32[]{:S(2)}, u32[]{:S(2)}) %collective-permute-start.2) | collective-permute-done | bytes 16928 | tf_op jit(solution)/shard_map/ppermute | solution.py:20
  28.2 0.8 copy-done.1
  30.6 30.1 %all-reduce.3 = (f32[]{:T(128)}, f32[128]{0:T(128)S(1)}, f32[128]{0:T(128)S(1)}) all-reduce(f32[]{:T(128)} %convert_reduce_fusion, f32[128]{0:T(128)S(1)} %get-tuple-element.55, f32[128]{0:T(128)S(1)} %get-tuple-element.54), channel_id=1, replica_groups=mesh['groups'=2,'space'=4,'batch'=4] {'space','batch'}, use_global_device_ids=true, to_apply=%region_3.4 | all-reduce | flops 257 | bytes 2056 | tf_op jit(solution)/shard_map/psum | solution.py:119
  61.6 3.6 %collective-permute-done.8 = bf16[1,8,128]{2,1,0:T(8,128)(2,1)S(1)} collective-permute-done((bf16[1,8,128]{2,1,0:T(8,128)(2,1)S(1)}, bf16[1,8,128]{2,1,0:T(8,128)(2,1)S(1)}, u32[]{:S(2)}, u32[]{:S(2)}) %collective-permute-start.8) | collective-permute-done | bytes 2080 | tf_op jit(solution)/shard_map/ppermute | solution.py:10
  65.2 4.5 %collective-permute-done.9 = bf16[1,8,128]{2,1,0:T(8,128)(2,1)S(1)} collective-permute-done((bf16[1,8,128]{2,1,0:T(8,128)(2,1)S(1)}, bf16[1,8,128]{2,1,0:T(8,128)(2,1)S(1)}, u32[]{:S(2)}, u32[]{:S(2)}) %collective-permute-start.9) | collective-permute-done | bytes 2080 | tf_op jit(solution)/shard_map/ppermute | solution.py:10
  69.9 2.0 collective-permute-start.10
  71.9 0.7 add_rsqrt_fusion
  72.5 1.1 collective-permute-done.11
  73.6 1.9 collective-permute-done.10
  75.9 0.7 copy-done
  78.9 0.6 copy-done.5
  79.5 0.3 fusion.192
  80.1 3.4 %collective-permute-done.4 = bf16[1,8,128]{2,1,0:T(8,128)(2,1)S(1)} collective-permute-done((bf16[1,8,128]{2,1,0:T(8,128)(2,1)S(1)}, bf16[1,8,128]{2,1,0:T(8,128)(2,1)S(1)}, u32[]{:S(2)}, u32[]{:S(2)}) %collective-permute-start.4) | collective-permute-done | bytes 2080 | tf_op jit(solution)/shard_map/ppermute | solution.py:10
  83.6 29.5 %all-reduce.2 = (f32[128]{0:T(128)S(1)}, f32[128]{0:T(128)S(1)}) all-reduce(f32[128]{0:T(128)S(1)} %get-tuple-element.57, f32[128]{0:T(128)S(1)} %get-tuple-element.56), channel_id=1, replica_groups=mesh['groups'=2,'space'=4,'batch'=4] {'space','batch'}, use_global_device_ids=true, to_apply=%region_9.10 | all-reduce | flops 256 | bytes 2048 | tf_op jit(solution)/shard_map/psum | solution.py:141
  113.3 2.0 collective-permute-start.6
  115.4 1.7 collective-permute-done.7
  117.0 1.9 collective-permute-done.6
  121.0 1.5 multiply_convert_fusion
  122.7 0.2 fusion.53
  122.9 0.3 fusion.51
  123.2 0.2 fusion.49
  123.4 0.3 fusion.47
  123.9 0.3 fusion.43
  124.2 0.3 fusion.41
  124.4 0.3 fusion.39
  124.7 1.2 copy.85
  126.0 0.2 fusion.35
  126.2 0.2 fusion.33
  126.5 0.2 fusion.31
  126.7 0.2 fusion.29
  127.0 0.2 fusion.27
  127.5 0.2 fusion.23
  127.7 0.2 fusion.21
  128.0 1.2 copy.86
  129.2 15.8 %reduce-scatter.3.cloned.1.call-done = bf16[9,128,32]{1,0,2:T(8,128)(2,1)} async-done(((bf16[9,128,128]{1,0,2:T(8,128)(2,1)}), bf16[9,128,32]{1,0,2:T(8,128)(2,1)}) %reduce-scatter.3.cloned.1.call-update) | async-done | bytes 73744 | tf_op jit(solution)/shard_map/reduce_scatter | solution.py:95
  145.0 24.3 %reduce-scatter.5.cloned.1.call-done = bf16[9,128,32]{1,0,2:T(8,128)(2,1)} async-done(((bf16[9,128,128]{1,0,2:T(8,128)(2,1)}), bf16[9,128,32]{1,0,2:T(8,128)(2,1)}) %reduce-scatter.5.cloned.1.call-update) | async-done | bytes 73744 | tf_op jit(solution)/shard_map/reduce_scatter | solution.py:95
  169.3 37.9 %all-reduce.7.cloned.1.call-done = (bf16[9,128,32]{1,0,2:T(8,128)(2,1)}, bf16[9,128,32]{1,0,2:T(8,128)(2,1)}) async-done(((bf16[9,128,32]{1,0,2:T(8,128)(2,1)}, bf16[9,128,32]{1,0,2:T(8,128)(2,1)}), (bf16[9,128,32]{1,0,2:T(8,128)(2,1)}, bf16[9,128,32]{1,0,2:T(8,128)(2,1)})) %all-reduce.7.cloned.1.call-update) | async-done | bytes 147472 | tf_op jit(solution)/shard_map/psum | solution.py:94
  207.3 1.6 copy.87
  208.9 0.7 copy.88
  (100 shorter events, 8.5 us)
Async XLA Ops:
  7.2 137.8 %reduce-scatter.3.cloned.1.call-start = ((), (), s32[]{:S(2)}) async-start(), calls=%async_computation.2 | async-start | bytes 655360 | tf_op jit(solution)/shard_map/reduce_scatter | solution.py:95
  9.0 7.7 %copy-start.4 = (s32[8,64]{1,0:T(8,128)S(1)}, s32[8,64]{1,0:T(8,128)}, u32[]{:S(2)}) copy-start(s32[8,64]{1,0:T(8,128)} %param.12) | copy-start | bytes 6148
  9.0 4.7 %collective-permute-start = (bf16[1,8,128]{2,1,0:T(8,128)(2,1)S(1)}, bf16[1,8,128]{2,1,0:T(8,128)(2,1)S(1)}, u32[]{:S(2)}, u32[]{:S(2)}) collective-permute-start(bf16[1,8,128]{2,1,0:T(8,128)(2,1)S(1)} %bitcast.514), channel_id=1, source_target_pairs={{0,4},{4,0},{8,12},{12,8},{1,5},{5,1},{9,13},{13,9},{2,6},{6,2},{1... | collective-permute-start | bytes 6152 | tf_op jit(solution)/shard_map/ppermute | solution.py:10
  13.6 4.6 %collective-permute-start.1 = (bf16[1,8,128]{2,1,0:T(8,128)(2,1)S(1)}, bf16[1,8,128]{2,1,0:T(8,128)(2,1)S(1)}, u32[]{:S(2)}, u32[]{:S(2)}) collective-permute-start(bf16[1,8,128]{2,1,0:T(8,128)(2,1)S(1)} %collective-permute-done), channel_id=1, source_target_pairs={{0,8},{4,12},{8,0},{12,4},{1,9},{5,13},{9,1},{13,5},{2,10},{6,14},... | collective-permute-start | bytes 6152 | tf_op jit(solution)/shard_map/ppermute | solution.py:10
  18.3 5.5 %collective-permute-start.3 = (bf16[1,1,66,128]{3,2,1,0:T(8,128)(2,1)S(1)}, bf16[1,1,66,128]{3,2,1,0:T(8,128)(2,1)S(1)}, u32[]{:S(2)}, u32[]{:S(2)}) collective-permute-start(bf16[1,1,66,128]{3,2,1,0:T(8,128)(2,1)S(1)} %get-tuple-element.94), channel_id=1, source_target_pairs={{4,0},{8,4},{12,8},{0,12},{5,1},{9,5},{13,9},{1,13},{6,2},{10,6},{... | collective-permute-start | bytes 50696 | tf_op jit(solution)/shard_map/ppermute | solution.py:21
  22.3 5.6 %collective-permute-start.2 = (bf16[1,1,66,128]{3,2,1,0:T(8,128)(2,1)S(1)}, bf16[1,1,66,128]{3,2,1,0:T(8,128)(2,1)S(1)}, u32[]{:S(2)}, u32[]{:S(2)}) collective-permute-start(bf16[1,1,66,128]{3,2,1,0:T(8,128)(2,1)S(1)} %get-tuple-element.95), channel_id=1, source_target_pairs={{0,4},{4,8},{8,12},{12,0},{1,5},{5,9},{9,13},{13,1},{2,6},{6,10},{... | collective-permute-start | bytes 50696 | tf_op jit(solution)/shard_map/ppermute | solution.py:20
  28.0 1.0 copy-start.1
  30.3 31.1 %copy-start.2 = (bf16[1,8,64,128]{3,2,1,0:T(8,128)(2,1)S(1)}, bf16[1,8,64,128]{3,2,1,0:T(8,128)(2,1)}, u32[]{:S(2)}) copy-start(bf16[1,8,64,128]{3,2,1,0:T(8,128)(2,1)} %param.17) | copy-start | bytes 393220
  61.6 3.7 %collective-permute-start.8 = (bf16[1,8,128]{2,1,0:T(8,128)(2,1)S(1)}, bf16[1,8,128]{2,1,0:T(8,128)(2,1)S(1)}, u32[]{:S(2)}, u32[]{:S(2)}) collective-permute-start(bf16[1,8,128]{2,1,0:T(8,128)(2,1)S(1)} %bitcast.515), channel_id=1, source_target_pairs={{0,4},{4,0},{8,12},{12,8},{1,5},{5,1},{9,13},{13,9},{2,6},{6,2},{1... | collective-permute-start | bytes 6152 | tf_op jit(solution)/shard_map/ppermute | solution.py:10
  65.2 4.5 %collective-permute-start.9 = (bf16[1,8,128]{2,1,0:T(8,128)(2,1)S(1)}, bf16[1,8,128]{2,1,0:T(8,128)(2,1)S(1)}, u32[]{:S(2)}, u32[]{:S(2)}) collective-permute-start(bf16[1,8,128]{2,1,0:T(8,128)(2,1)S(1)} %collective-permute-done.8), channel_id=1, source_target_pairs={{0,8},{4,12},{8,0},{12,4},{1,9},{5,13},{9,1},{13,5},{2,10},{6,14},... | collective-permute-start | bytes 6152 | tf_op jit(solution)/shard_map/ppermute | solution.py:10
  69.8 3.8 %collective-permute-start.11 = (bf16[1,1,66,128]{3,2,1,0:T(8,128)(2,1)S(1)}, bf16[1,1,66,128]{3,2,1,0:T(8,128)(2,1)S(1)}, u32[]{:S(2)}, u32[]{:S(2)}) collective-permute-start(bf16[1,1,66,128]{3,2,1,0:T(8,128)(2,1)S(1)} %get-tuple-element.91), channel_id=1, source_target_pairs={{4,0},{8,4},{12,8},{0,12},{5,1},{9,5},{13,9},{1,13},{6,2},{10,6},{... | collective-permute-start | bytes 50696 | tf_op jit(solution)/shard_map/ppermute | solution.py:21
  69.9 5.6 %collective-permute-start.10 = (bf16[1,1,66,128]{3,2,1,0:T(8,128)(2,1)S(1)}, bf16[1,1,66,128]{3,2,1,0:T(8,128)(2,1)S(1)}, u32[]{:S(2)}, u32[]{:S(2)}) collective-permute-start(bf16[1,1,66,128]{3,2,1,0:T(8,128)(2,1)S(1)} %get-tuple-element.90), channel_id=1, source_target_pairs={{0,4},{4,8},{8,12},{12,0},{1,5},{5,9},{9,13},{13,1},{2,6},{6,10},{... | collective-permute-start | bytes 50696 | tf_op jit(solution)/shard_map/ppermute | solution.py:20
  75.6 1.0 copy-start
  78.8 0.7 copy-start.5
  78.8 0.7 copy-start.6
  79.8 3.7 %collective-permute-start.4 = (bf16[1,8,128]{2,1,0:T(8,128)(2,1)S(1)}, bf16[1,8,128]{2,1,0:T(8,128)(2,1)S(1)}, u32[]{:S(2)}, u32[]{:S(2)}) collective-permute-start(bf16[1,8,128]{2,1,0:T(8,128)(2,1)S(1)} %bitcast.516), channel_id=1, source_target_pairs={{0,4},{4,0},{8,12},{12,8},{1,5},{5,1},{9,13},{13,9},{2,6},{6,2},{1... | collective-permute-start | bytes 6152 | tf_op jit(solution)/shard_map/ppermute | solution.py:10
  83.5 29.6 %collective-permute-start.5 = (bf16[1,8,128]{2,1,0:T(8,128)(2,1)S(1)}, bf16[1,8,128]{2,1,0:T(8,128)(2,1)S(1)}, u32[]{:S(2)}, u32[]{:S(2)}) collective-permute-start(bf16[1,8,128]{2,1,0:T(8,128)(2,1)S(1)} %collective-permute-done.4), channel_id=1, source_target_pairs={{0,8},{4,12},{8,0},{12,4},{1,9},{5,13},{9,1},{13,5},{2,10},{6,14},... | collective-permute-start | bytes 6152 | tf_op jit(solution)/shard_map/ppermute | solution.py:10
  113.1 7.9 %copy-start.7 = (f32[128]{0:T(128)}, f32[128]{0:T(128)S(1)}, u32[]{:S(2)}) copy-start(f32[128]{0:T(128)S(1)} %get-tuple-element.58) | copy-start | bytes 1540
  113.1 7.9 %copy-start.8 = (f32[128]{0:T(128)}, f32[128]{0:T(128)S(1)}, u32[]{:S(2)}) copy-start(f32[128]{0:T(128)S(1)} %get-tuple-element.59) | copy-start | bytes 1540
  113.2 3.8 %collective-permute-start.7 = (bf16[1,1,66,128]{3,2,1,0:T(8,128)(2,1)S(1)}, bf16[1,1,66,128]{3,2,1,0:T(8,128)(2,1)S(1)}, u32[]{:S(2)}, u32[]{:S(2)}) collective-permute-start(bf16[1,1,66,128]{3,2,1,0:T(8,128)(2,1)S(1)} %get-tuple-element.92), channel_id=1, source_target_pairs={{4,0},{8,4},{12,8},{0,12},{5,1},{9,5},{13,9},{1,13},{6,2},{10,6},{... | collective-permute-start | bytes 50696 | tf_op jit(solution)/shard_map/ppermute | solution.py:21
  113.3 5.6 %collective-permute-start.6 = (bf16[1,1,66,128]{3,2,1,0:T(8,128)(2,1)S(1)}, bf16[1,1,66,128]{3,2,1,0:T(8,128)(2,1)S(1)}, u32[]{:S(2)}, u32[]{:S(2)}) collective-permute-start(bf16[1,1,66,128]{3,2,1,0:T(8,128)(2,1)S(1)} %get-tuple-element.93), channel_id=1, source_target_pairs={{0,4},{4,8},{8,12},{12,0},{1,5},{5,9},{9,13},{13,1},{2,6},{6,10},{... | collective-permute-start | bytes 50696 | tf_op jit(solution)/shard_map/ppermute | solution.py:20
  125.9 43.4 %reduce-scatter.5.cloned.1.call-start = ((), (), s32[]{:S(2)}) async-start(), calls=%async_computation.3 | async-start | bytes 655360 | tf_op jit(solution)/shard_map/reduce_scatter | solution.py:95
  129.2 78.1 %all-reduce.7.cloned.1.call-start = ((), (), s32[]{:S(2)}) async-start(), calls=%async_computation.4 | async-start | bytes 524288 | tf_op jit(solution)/shard_map/psum | solution.py:94
  207.3 1.6 copy-start.3
Sparse Core Ops, SparseCore 0:
  126.0 18.9 reduce-scatter.2
  147.6 21.6 reduce-scatter.4
  171.7 35.5 all-reduce.6
where the time goes:
time: 216 us
  waiting for transfers between devices  104 us (48%)
  blocking collectives  59.6 us (28%)
  between operations  15 us (7%)
  starting transfers between devices  14.7 us (7%)
  matrix products  9.61 us (4%)
  local copies, waits for them, and re-layouts  7.76 us (4%)
  other arithmetic  5.5 us (3%)
    reduce_scatter x2, waiting for transfers between devices, reduce_weights(): lax.psum_scatter(summed, 'batch', scatter_dimension=2, tiled=True)  40.1 us
    psum x1, waiting for transfers between devices, reduce_weights(): summed = lax.psum(partial_grad.astype(jnp.bfloat16), 'space')  37.9 us
    psum x1, blocking collectives, body(): lax.psum((jnp.sum(first_features * ocean_mask, axis=(0, 1, 2)), jnp.sum(f...  30.1 us
    psum x1, blocking collectives, body(): lax.psum((jnp.sum(preactivation_gradient, axis=(0, 1, 2)), jnp.sum(preact...  29.5 us
    ppermute x6, waiting for transfers between devices, partner(): return lax.ppermute(value, axis, pairs)  13.9 us
    ppermute x3, waiting for transfers between devices, extended_2(): before = lax.ppermute(last, axis, up)  7.82 us
    ppermute x6, starting transfers between devices, partner(): return lax.ppermute(value, axis, pairs)  6.43 us
    unnamed x24, local copies, waits for them, and re-layouts  4.49 us
  transfers between devices with their start and end apart: 15, of which 14 were waited for; matrix products, arithmetic and copies ran while one was open for 2% of the time, Pallas kernels for 0%

commit v1 on v0

v1 whole, which is shorter than its diff:
```python
import functools

import jax
import jax.numpy as jnp
from jax import lax
from jax.experimental import pallas as pl
from jax.experimental.pallas import tpu as pltpu
from jax.sharding import PartitionSpec as P

F32 = jnp.float32
BF16 = jnp.bfloat16


def gelu_parts(value):
    inner = 0.7978845608 * (value + 0.044715 * value * value * value)
    hyper = jnp.tanh(inner)
    act = 0.5 * value * (1.0 + hyper)
    slope = 0.5 * (1.0 + hyper) + 0.5 * value * (1.0 - hyper * hyper) * 0.7978845608 * (
        1.0 + 3.0 * 0.044715 * value * value
    )
    return act, slope


def kernel(
    nz, nb, lon, lat, ch, units,
    fields, land, w_in, w_out, gain, offset, target,
    output, grad_in, grad_out, gain_gradient, offset_gradient,
    mask, first, dact, dpre, s_in, s_act, s_dout, w_back, dout_t,
    rows1, head1, tail1, west1, east1,
    rows2, head2, tail2, west2, east2,
    stats1, stats2,
    part_a, pair_a, half_a, cross_a, mine_a, ring_a, full_a,
    part_b, pair_b, half_b, cross_b, mine_b, ring_b, full_b,
    row_sems, col_sems, stat_sems, pair_sems, cross_sems, ring_sems, full_sems,
):
    nd = nz * nb
    nx = nb // 2
    cells = lon * lat
    z = lax.axis_index("space")
    b = lax.axis_index("batch")
    me = z * nb + b
    core = lax.rem(b, 2)
    col = b // 2
    other = 1 - core

    def device(zz, bb):
        return {"space": zz, "batch": bb}

    def copy(src, dst, send, recv, zz, bb):
        return pltpu.make_async_remote_copy(
            src_ref=src, dst_ref=dst, send_sem=send, recv_sem=recv,
            device_id=device(zz, bb), device_id_type=pl.DeviceIdType.MESH,
        )

    def over(count, fn):
        def step(k, carry):
            fn(k)
            return carry
        lax.fori_loop(1, count, step, 0)

    def row_copy(which, buf, slot, zz):
        return copy(buf.at[slot], buf.at[slot], row_sems.at[which, 0, zz],
                    row_sems.at[which, 1, slot], zz, b)

    def send_rows(which, buf):
        over(nz, lambda k: row_copy(which, buf, z, lax.rem(z + k, nz)).start())

    def recv_rows(which, buf):
        def one(k):
            src = lax.rem(z + k, nz)
            row_copy(which, buf, src, src).wait_recv()
        over(nz, one)

    def drain_rows(which, buf):
        over(nz, lambda k: row_copy(which, buf, z, lax.rem(z + k, nz)).wait_send())

    up = lax.rem(z + 1, nz)
    down = lax.rem(z + nz - 1, nz)

    def col_copies(which, head, tail, west, east):
        return (
            copy(head, east, col_sems.at[which, 0, 0], col_sems.at[which, 1, 0], down, b),
            copy(tail, west, col_sems.at[which, 0, 1], col_sems.at[which, 1, 1], up, b),
        )

    def stat_copy(which, buf, slot, peer):
        return copy(buf.at[slot], buf.at[slot], stat_sems.at[which, 0, peer],
                    stat_sems.at[which, 1, slot], peer // nb, lax.rem(peer, nb))

    def send_stats(which, buf):
        over(nd, lambda k: stat_copy(which, buf, me, lax.rem(me + k, nd)).start())

    def recv_stats(which, buf):
        def one(k):
            src = lax.rem(me + k, nd)
            stat_copy(which, buf, src, src).wait_recv()
        over(nd, one)

    def drain_stats(which, buf):
        over(nd, lambda k: stat_copy(which, buf, me, lax.rem(me + k, nd)).wait_send())

    barrier = pltpu.get_barrier_semaphore()

    def greet(k):
        peer = lax.rem(me + k, nd)
        pl.semaphore_signal(barrier, inc=1, device_id=device(peer // nb, lax.rem(peer, nb)),
                            device_id_type=pl.DeviceIdType.MESH)
    over(nd, greet)

    row_id = lax.broadcasted_iota(jnp.int32, (lat, ch), 0)
    zero_row = jnp.zeros((1, ch), F32)

    land_f = land[...].astype(F32)
    diagonal = lax.broadcasted_iota(jnp.int32, (lat, lat), 0) == lax.broadcasted_iota(
        jnp.int32, (lat, lat), 1)
    spread = jnp.concatenate(
        [jnp.where(diagonal, land_f[i:i + 1, :], 0.0) for i in range(lon)], axis=0)
    mask[...] = jnp.dot(spread.astype(BF16), jnp.ones((lat, ch), BF16), preferred_element_type=F32)

    def at(i):
        return pl.ds(i * lat, lat)

    def shift_up(v, ghost):
        return jnp.concatenate([v[1:], ghost], axis=0)

    def shift_down(v):
        return jnp.concatenate([zero_row, v[:-1]], axis=0)

    def put(s, i, v, lane):
        s[i, :, lane * ch:(lane + 1) * ch] = v.astype(BF16)

    masked = [fields[0, i].astype(F32) * mask[at(i)] for i in range(lon)]
    seen = [target[0, i].astype(F32) * mask[at(i)] for i in range(lon)]
    halves = []
    for h in range(2):
        half = mask[h * cells // 2:(h + 1) * cells // 2]
        halves.append(jnp.broadcast_to(jnp.sum(half, axis=0, keepdims=True), (8, ch)))
    rows1[z] = jnp.concatenate(
        [v[lat - 1:] for v in masked] + [v[lat - 1:] for v in seen] + halves, axis=0).astype(BF16)
    head1[0:lat] = masked[0].astype(BF16)
    head1[lat:2 * lat] = seen[0].astype(BF16)
    tail1[0:lat] = masked[-1].astype(BF16)
    tail1[lat:2 * lat] = seen[-1].astype(BF16)

    pl.semaphore_wait(barrier, nd - 1)
    send_rows(0, rows1)
    cols1 = col_copies(0, head1, tail1, west1, east1)
    for c in cols1:
        c.start()

    for i in range(lon):
        put(s_in, i + 1, shift_down(masked[i]), 0)
        put(s_in, i + 1, masked[i], 1)
    for tap in range(9):
        f, s = tap // 3, tap % 3
        w = w_out[f, s * ch:(s + 1) * ch, :].astype(F32)
        w_back[f, s * ch:(s + 1) * ch, :] = w.T.astype(BF16)

    for c in cols1:
        c.wait_recv()
    recv_rows(0, rows1)

    opposite = nz - 1 - z
    beyond = lax.rem(nz - z, nz)
    before = lax.rem(2 * nz - 2 - z, nz)

    def ghosts(buf, start):
        facing = buf[opposite].astype(F32)
        left = buf[beyond].astype(F32)[start:start + 1]
        right = buf[before].astype(F32)[start + lon - 1:start + lon]
        return [left] + [facing[start + lon - 1 - i:start + lon - i] for i in range(lon)] + [right]

    ghost_in = ghosts(rows1, 0)
    edge_w = west1[0:lat].astype(F32)
    edge_e = east1[0:lat].astype(F32)
    for i, v in ((0, edge_w), (lon + 1, edge_e)):
        put(s_in, i, shift_down(v), 0)
        put(s_in, i, v, 1)
    for i in range(lon + 2):
        v = edge_w if i == 0 else edge_e if i == lon + 1 else (
            fields[0, i - 1].astype(F32) * mask[at(i - 1)])
        put(s_in, i, shift_up(v, ghost_in[i]), 2)

    def window(s, f):
        return s[f:f + lon].reshape(cells, 3 * ch)

    total = jnp.dot(window(s_in, 0), w_in[0], preferred_element_type=F32)
    total += jnp.dot(window(s_in, 1), w_in[1], preferred_element_type=F32)
    total += jnp.dot(window(s_in, 2), w_in[2], preferred_element_type=F32)
    rounded = total.astype(BF16).astype(F32)
    first[...] = rounded
    held = rounded * mask[...]
    stats1[me, 0:1] = jnp.sum(held, axis=0, keepdims=True)
    stats1[me, 1:2] = jnp.sum(held * rounded, axis=0, keepdims=True)
    send_stats(0, stats1)

    count = zero_row
    for k in range(nz):
        packet = rows1[k].astype(F32)
        count = count + packet[16:17] + packet[24:25]
    count = count * float(nb)
    scale = lax.rsqrt(count)

    def scaled(v):
        return (v * scale).astype(BF16).astype(F32)

    for i in range(lon + 2):
        if i == 0:
            v = west1[lat:2 * lat].astype(F32)
        elif i == lon + 1:
            v = east1[lat:2 * lat].astype(F32)
        else:
            v = target[0, i - 1].astype(F32) * mask[at(i - 1)]
        v = scaled(v)
        put(s_dout, i, shift_up(v, zero_row), 0)
        put(s_dout, i, v, 1)
        put(s_dout, i, shift_down(v), 2)
        if 0 < i <= lon and i % 2 == 0:
            pair = jnp.concatenate([earlier, v], axis=0)
            dout_t[:, (i - 2) * lat:i * lat] = pair.T.astype(BF16)
        earlier = v
    ghost_dout = [scaled(v) for v in ghosts(rows1, lon)]
    total = jnp.dot(window(s_dout, 2), w_back[0], preferred_element_type=F32)
    total += jnp.dot(window(s_dout, 1), w_back[1], preferred_element_type=F32)
    total += jnp.dot(window(s_dout, 0), w_back[2], preferred_element_type=F32)
    extra = jnp.zeros((2 * lon, ch), F32)
    for f in range(3):
        piece = jnp.concatenate(ghost_dout[f:f + lon] + [jnp.zeros((lon, ch), F32)], axis=0)
        extra += jnp.dot(piece.astype(BF16), w_back[f, 2 * ch:3 * ch, :], preferred_element_type=F32)
    for i in range(lon):
        dact[at(i)] = total[i * lat:(i + 1) * lat] + jnp.where(
            row_id == lat - 1, extra[i:i + 1], 0.0)

    recv_stats(0, stats1)

    def gathered(buf):
        acc = buf[0]
        for k in range(1, nd):
            acc = acc + buf[k]
        return acc

    acc = gathered(stats1)
    mean = acc[0:1] / count
    var = acc[1:2] / count - mean * mean
    inverse = lax.rsqrt(var + 1e-05)
    gains = gain[...]
    offsets = offset[...]

    sum_off = zero_row
    sum_gain = zero_row
    last = []
    for i in range(lon):
        xhat = (first[at(i)] - mean) * inverse
        act, slope = gelu_parts(gains * xhat + offsets)
        act = (act * mask[at(i)]).astype(BF16)
        d = dact[at(i)] * mask[at(i)] * slope
        dpre[at(i)] = d
        sum_off += jnp.sum(d, axis=0, keepdims=True)
        sum_gain += jnp.sum(d * xhat, axis=0, keepdims=True)
        s_act[i + 1, :, ch:2 * ch] = act
        last.append(act.astype(F32)[lat - 1:])
        if i == 0:
            head2[...] = act
        if i == lon - 1:
            tail2[...] = act
    stats2[me, 0:1] = sum_off
    stats2[me, 1:2] = sum_gain
    send_stats(1, stats2)
    rows2[z] = jnp.concatenate(last + [jnp.zeros((lon, ch), F32)], axis=0).astype(BF16)
    cols2 = col_copies(1, head2, tail2, west2, east2)
    for c in cols2:
        c.start()
    send_rows(1, rows2)

    for i in range(1, lon + 1):
        put(s_act, i, shift_down(s_act[i, :, ch:2 * ch].astype(F32)), 0)
    for c in cols2:
        c.wait_recv()
    recv_rows(1, rows2)
    ghost_act = ghosts(rows2, 0)
    s_act[0, :, ch:2 * ch] = west2[...]
    s_act[lon + 1, :, ch:2 * ch] = east2[...]
    for i in range(lon + 2):
        v = s_act[i, :, ch:2 * ch].astype(F32)
        if i == 0 or i == lon + 1:
            put(s_act, i, shift_down(v), 0)
        put(s_act, i, shift_up(v, ghost_act[i]), 2)

    share = ch // nb
    live = 9 * share
    padded = units * 16 * nz

    def tap_grad(s, d_t, part):
        for f in range(3):
            g = jnp.dot(d_t, window(s, f), preferred_element_type=F32).astype(BF16)
            for t in range(3):
                tap = 3 * f + t
                for k in range(nb):
                    part[k % 2, k // 2, tap * share:(tap + 1) * share, :] = (
                        g[k * share:(k + 1) * share, t * ch:(t + 1) * ch])
        if padded > live:
            for k in range(nb):
                part[k % 2, k // 2, live:padded, :] = jnp.zeros((padded - live, ch), BF16)

    def pair_copy(which, part, pair):
        return copy(part.at[other], pair, pair_sems.at[which, 0], pair_sems.at[which, 1],
                    z, 2 * col + other)

    def cross_copy(which, half, cross, slot, peer, x):
        return copy(half.at[peer], cross.at[slot], cross_sems.at[which, 0, peer],
                    cross_sems.at[which, 1, slot], z, 2 * x + core)

    def ring_copy(which, mine, ring, slot, peer):
        return copy(mine.at[peer], ring.at[slot], ring_sems.at[which, 0, peer],
                    ring_sems.at[which, 1, slot], peer, b)

    def full_copy(which, full, slot, peer):
        return copy(full.at[slot], full.at[slot], full_sems.at[which, 0, peer],
                    full_sems.at[which, 1, slot], peer, b)

    def after_pair(which, part, pair, half, cross):
        pair_copy(which, part, pair).wait_recv()
        for x in range(nx):
            half[x] = (part[core, x].astype(F32) + pair[x].astype(F32)).astype(BF16)

        def one(k):
            x = lax.rem(col + k, nx)
            cross_copy(which, half, cross, col, x, x).start()
        over(nx, one)

    def after_cross(which, half, cross, mine, ring):
        acc = half[col].astype(F32)
        for k in range(1, nx):
            x = lax.rem(col + k, nx)
            cross_copy(which, half, cross, x, x, x).wait_recv()
            acc = acc + cross[x].astype(F32)
        for k in range(nz):
            mine[k] = acc[k * units * 16:(k + 1) * units * 16].astype(BF16)

        def one(k):
            peer = lax.rem(z + k, nz)
            ring_copy(which, mine, ring, z, peer).start()
        over(nz, one)

    def after_ring(which, mine, ring, full):
        acc = mine[z].astype(F32)
        for k in range(1, nz):
            src = lax.rem(z + k, nz)
            ring_copy(which, mine, ring, src, src).wait_recv()
            acc = acc + ring[src].astype(F32)
        full[z] = acc.astype(BF16)

        def one(k):
            full_copy(which, full, z, lax.rem(z + k, nz)).start()
        over(nz, one)

    def after_full(which, full, out):
        def one(k):
            src = lax.rem(z + k, nz)
            full_copy(which, full, src, src).wait_recv()
        over(nz, one)
        out[...] = full[...].reshape(padded, ch)[0:live].astype(F32)

    def drain(which, part, pair, half, cross, mine, ring, full):
        pair_copy(which, part, pair).wait_send()

        def one_x(k):
            x = lax.rem(col + k, nx)
            cross_copy(which, half, cross, col, x, x).wait_send()
        over(nx, one_x)

        def one_z(k):
            peer = lax.rem(z + k, nz)
            ring_copy(which, mine, ring, z, peer).wait_send()
            full_copy(which, full, z, peer).wait_send()
        over(nz, one_z)

    tap_grad(s_act, dout_t[...], part_a)
    pair_copy(0, part_a, pair_a).start()

    recv_stats(1, stats2)
    acc = gathered(stats2)
    off_total = acc[0:1]
    gain_total = acc[1:2]
    offset_gradient[...] = off_total
    gain_gradient[...] = gain_total
    for i in range(0, lon, 2):
        pieces = []
        for j in (i, i + 1):
            xhat = (first[at(j)] - mean) * inverse
            pieces.append(mask[at(j)] * gains * inverse * (
                dpre[at(j)] - (off_total + xhat * gain_total) / count))
        pair = jnp.concatenate(pieces, axis=0)
        dout_t[:, i * lat:(i + 2) * lat] = pair.T.astype(BF16)
    tap_grad(s_in, dout_t[...], part_b)
    pair_copy(1, part_b, pair_b).start()

    after_pair(0, part_a, pair_a, half_a, cross_a)
    after_pair(1, part_b, pair_b, half_b, cross_b)

    total = jnp.dot(window(s_act, 0), w_out[0], preferred_element_type=F32)
    total += jnp.dot(window(s_act, 1), w_out[1], preferred_element_type=F32)
    total += jnp.dot(window(s_act, 2), w_out[2], preferred_element_type=F32)
    output[0] = (total * mask[...]).astype(BF16).reshape(lon, lat, ch)

    after_cross(0, half_a, cross_a, mine_a, ring_a)
    after_cross(1, half_b, cross_b, mine_b, ring_b)
    after_ring(0, mine_a, ring_a, full_a)
    after_ring(1, mine_b, ring_b, full_b)
    after_full(0, full_a, grad_out)
    after_full(1, full_b, grad_in)

    for c in cols1 + cols2:
        c.wait_send()
    drain_rows(0, rows1)
    drain_rows(1, rows2)
    drain_stats(0, stats1)
    drain_stats(1, stats2)
    drain(0, part_a, pair_a, half_a, cross_a, mine_a, ring_a, full_a)
    drain(1, part_b, pair_b, half_b, cross_b, mine_b, ring_b, full_b)


def body(nz, nb, fields, land, conv_in, conv_out, gain, offset, target):
    lon, lat, ch = fields.shape[1:]
    nd = nz * nb
    nx = nb // 2
    share = ch // nb
    units = -(-(9 * share // 16) // nz)
    padded = units * 16 * nz
    vm = pltpu.VMEM
    reduction = [
        vm((2, nx, padded, ch), BF16),
        vm((nx, padded, ch), BF16),
        vm((nx, padded, ch), BF16),
        vm((nx, padded, ch), BF16),
        vm((nz, units * 16, ch), BF16),
        vm((nz, units * 16, ch), BF16),
        vm((nz, units * 16, ch), BF16),
    ]
    dma = pltpu.SemaphoreType.DMA
    scratch = [
        vm((lon * lat, ch), F32),
        vm((lon * lat, ch), F32),
        vm((lon * lat, ch), F32),
        vm((lon * lat, ch), F32),
        vm((lon + 2, lat, 3 * ch), BF16),
        vm((lon + 2, lat, 3 * ch), BF16),
        vm((lon + 2, lat, 3 * ch), BF16),
        vm((3, 3 * ch, ch), BF16),
        vm((ch, lon * lat), BF16),
        vm((nz, 32, ch), BF16),
        vm((2 * lat, ch), BF16), vm((2 * lat, ch), BF16),
        vm((2 * lat, ch), BF16), vm((2 * lat, ch), BF16),
        vm((nz, 16, ch), BF16),
        vm((lat, ch), BF16), vm((lat, ch), BF16),
        vm((lat, ch), BF16), vm((lat, ch), BF16),
        vm((nd, 8, ch), F32),
        vm((nd, 8, ch), F32),
        *reduction,
        *reduction,
        dma((2, 2, nz)),
        dma((2, 2, 2)),
        dma((2, 2, nd)),
        dma((2, 2)),
        dma((2, 2, nx)),
        dma((2, 2, nz)),
        dma((2, 2, nz)),
    ]
    spec = pl.BlockSpec(memory_space=pltpu.VMEM)
    out, grad_in, grad_out, gain_gradient, offset_gradient = pl.pallas_call(
        functools.partial(kernel, nz, nb, lon, lat, ch, units),
        out_shape=(
            jax.ShapeDtypeStruct(fields.shape, BF16),
            jax.ShapeDtypeStruct((9 * share, ch), F32),
            jax.ShapeDtypeStruct((9 * share, ch), F32),
            jax.ShapeDtypeStruct((1, ch), F32),
            jax.ShapeDtypeStruct((1, ch), F32),
        ),
        in_specs=[spec] * 7,
        out_specs=(spec,) * 5,
        scratch_shapes=scratch,
        compiler_params=pltpu.CompilerParams(
            collective_id=0, has_side_effects=True, vmem_limit_bytes=40 * 1024 * 1024
        ),
    )(
        fields, land,
        conv_in.reshape(3, 3 * ch, ch), conv_out.reshape(3, 3 * ch, ch),
        gain.reshape(1, ch), offset.reshape(1, ch), target,
    )

    def taps(g):
        return g.reshape(9, share, ch).transpose(0, 2, 1)

    return (out, taps(grad_in), taps(grad_out),
            gain_gradient.reshape(ch), offset_gradient.reshape(ch))


def solution(mesh):
    in_specs = (
        P(("groups", "batch"), "space", None, None),
        P("space", None),
        P(),
        P(),
        P(),
        P(),
        P(("groups", "batch"), "space", None, None),
    )
    out_specs = (
        P(("groups", "batch"), "space", None, None),
        P("groups", None, "batch"),
        P("groups", None, "batch"),
        P("groups"),
        P("groups"),
    )
    step = functools.partial(body, mesh.shape["space"], mesh.shape["batch"])
    return jax.shard_map(step, mesh=mesh, in_specs=in_specs, out_specs=out_specs, check_vma=False)
```

time: 216 us -> 45 us (0.21)
  waiting for transfers between devices: 104 us -> 0 us
  blocking collectives: 59.6 us -> 0 us
  Pallas kernels: 0 us -> 36.6 us
  starting transfers between devices: 14.7 us -> 0 us
  between operations: 15 us -> 0.67 us
  matrix products: 9.61 us -> 0 us
  other arithmetic: 5.5 us -> 0 us
    psum x2 -> x0, blocking collectives: 59.6 us -> none  [the longest x1 30.1 us: body(): lax.psum((jnp.sum(first_features * ocean_mask, axis=(0, 1, 2)), jnp.sum(f...]
    reduce_scatter x2 -> x0, waiting for transfers between devices: 40.1 us -> none  [reduce_weights(): lax.psum_scatter(summed, 'batch', scatter_dimension=2, tiled=True)]
    psum x1 -> x0, waiting for transfers between devices: 37.9 us -> none  [reduce_weights(): summed = lax.psum(partial_grad.astype(jnp.bfloat16), 'space')]
    pallas_call x0 -> x1, Pallas kernels: none -> 36.6 us  [body(): pl.pallas_call(functools.partial(kernel, nz, nb, lon, lat, ch, units), ou...]
    ppermute x12 -> x0, waiting for transfers between devices: 25.8 us -> none  [the longest x6 13.9 us: partner(): return lax.ppermute(value, axis, pairs)]
    ppermute x12 -> x0, starting transfers between devices: 14.6 us -> none  [the longest x6 6.43 us: partner(): return lax.ppermute(value, axis, pairs)]
    dot_general x48 -> x0, matrix products: 9.61 us -> none  [the longest x18 4.41 us: tap_grads(): lax.dot_general(piece, flat, (((0,), (0,)), ((), ())), preferred_element_...]
    unnamed x24 -> x19, local copies, waits for them, and re-layouts: 4.49 us -> 7.4 us
  transfers between devices with their start and end apart: 15 -> 0, of which waited for: 14 -> 0; matrix products, arithmetic and copies ran while one was open for 2% -> 0% of each run, Pallas kernels for 0% -> 0%
where the time goes in v1:
time: 45 us; the launch traced here: 44.7 us
  Pallas kernels  36.6 us (81%)
  local copies, waits for them, and re-layouts  7.4 us (16%)
  between operations  0.67 us (1%)
    pallas_call x1, Pallas kernels, body(): pl.pallas_call(functools.partial(kernel, nz, nb, lon, lat, ch, units), ou...  36.6 us
    unnamed x19, local copies, waits for them, and re-layouts  7.4 us

profile of v1, /device:TPU:0, one launch (start us, length us, event | category | flops | bytes accessed | tf_op | source)
XLA Modules:
  0.0 44.7 jit_solution(16490354026334095852)
XLA Ops:
  0.6 0.0 copy-start.4
  0.6 0.0 copy-start.5
  0.7 0.0 copy-start.6
  0.7 0.7 %copy-done.4 = s32[8,64]{1,0:T(8,128)S(1)} copy-done((s32[8,64]{1,0:T(8,128)S(1)}, s32[8,64]{1,0:T(8,128)}, u32[]{:S(2)}) %copy-start.4) | copy-done | bytes 2072
  1.3 0.0 copy-done.5
  1.3 0.0 copy-done.6
  1.3 0.0 copy-start
  1.3 1.0 %copy-done = bf16[9,128,128]{2,1,0:T(8,128)(2,1)S(1)} copy-done((bf16[9,128,128]{2,1,0:T(8,128)(2,1)S(1)}, bf16[9,128,128]{2,1,0:T(8,128)(2,1)}, u32[]{:S(2)}) %copy-start) | copy-done | bytes 294936
  2.3 0.0 copy-start.1
  2.3 1.0 %copy-done.1 = bf16[9,128,128]{2,1,0:T(8,128)(2,1)S(1)} copy-done((bf16[9,128,128]{2,1,0:T(8,128)(2,1)S(1)}, bf16[9,128,128]{2,1,0:T(8,128)(2,1)}, u32[]{:S(2)}) %copy-start.1) | copy-done | bytes 294936
  3.3 0.0 copy-start.2
  3.3 0.9 %copy-done.2 = bf16[1,8,64,128]{3,2,1,0:T(8,128)(2,1)S(1)} copy-done((bf16[1,8,64,128]{3,2,1,0:T(8,128)(2,1)S(1)}, bf16[1,8,64,128]{3,2,1,0:T(8,128)(2,1)}, u32[]{:S(2)}) %copy-start.2) | copy-done | bytes 131096
  4.2 0.0 copy-start.3
  4.2 0.9 %copy-done.3 = bf16[1,8,64,128]{3,2,1,0:T(8,128)(2,1)S(1)} copy-done((bf16[1,8,64,128]{3,2,1,0:T(8,128)(2,1)S(1)}, bf16[1,8,64,128]{3,2,1,0:T(8,128)(2,1)}, u32[]{:S(2)}) %copy-start.3) | copy-done | bytes 131096
  5.1 36.6 %shard_map.110 = (bf16[1,8,64,128]{3,2,1,0:T(8,128)(2,1)S(1)}, f32[288,128]{1,0:T(8,128)S(1)}, f32[288,128]{1,0:T(8,128)S(1)}, f32[1,128]{1,0:T(1,128)S(1)}, f32[1,128]{1,0:T(1,128)S(1)}) custom-call(bf16[1,8,64,128]{3,2,1,0:T(8,128)(2,1)S(1)} %copy-done.2, s32[8,64]{1,0:T(8,128)S(1)} %copy-done.4, bf16[3,384,128]{2,1,0:T(8,128)(2,1)S(1)} %bitcast.12, ...), custom_call_target="tpu_custom_call" | custom-call | tf_op jit(solution)/shard_map/pallas_call | solution.py:470
  41.7 0.7 %copy.17 = bf16[1,8,64,128]{3,2,1,0:T(8,128)(2,1)} copy(bf16[1,8,64,128]{3,2,1,0:T(8,128)(2,1)S(1)} %get-tuple-element.20) | data formatting | bytes 262144
  42.4 0.7 %copy.18 = f32[9,128,32]{1,2,0:T(8,128)} copy(f32[9,128,32]{1,2,0:T(8,128)S(1)} %bitcast.15) | data formatting | bytes 294912
  43.0 0.7 %copy.19 = f32[9,128,32]{1,2,0:T(8,128)} copy(f32[9,128,32]{1,2,0:T(8,128)S(1)} %bitcast.14) | data formatting | bytes 294912
  43.7 0.5 %copy.20 = f32[128]{0:T(128)} copy(f32[128]{0:T(128)S(1)} %bitcast.19) | data formatting | bytes 1024
  44.2 0.5 %copy.21 = f32[128]{0:T(128)} copy(f32[128]{0:T(128)S(1)} %bitcast.18) | data formatting | bytes 1024
Async XLA Ops:
  0.6 0.7 %copy-start.4 = (s32[8,64]{1,0:T(8,128)S(1)}, s32[8,64]{1,0:T(8,128)}, u32[]{:S(2)}) copy-start(s32[8,64]{1,0:T(8,128)} %land.1) | copy-start | bytes 6148
  0.6 0.7 %copy-start.5 = (f32[128]{0:T(128)S(1)}, f32[128]{0:T(128)}, u32[]{:S(2)}) copy-start(f32[128]{0:T(128)} %param.11) | copy-start | bytes 1540
  0.7 0.7 %copy-start.6 = (f32[128]{0:T(128)S(1)}, f32[128]{0:T(128)}, u32[]{:S(2)}) copy-start(f32[128]{0:T(128)} %param.12) | copy-start | bytes 1540
  1.3 1.0 %copy-start = (bf16[9,128,128]{2,1,0:T(8,128)(2,1)S(1)}, bf16[9,128,128]{2,1,0:T(8,128)(2,1)}, u32[]{:S(2)}) copy-start(bf16[9,128,128]{2,1,0:T(8,128)(2,1)} %param.9) | copy-start | bytes 884740
  2.3 1.0 %copy-start.1 = (bf16[9,128,128]{2,1,0:T(8,128)(2,1)S(1)}, bf16[9,128,128]{2,1,0:T(8,128)(2,1)}, u32[]{:S(2)}) copy-start(bf16[9,128,128]{2,1,0:T(8,128)(2,1)} %param.10) | copy-start | bytes 884740
  3.3 0.9 %copy-start.2 = (bf16[1,8,64,128]{3,2,1,0:T(8,128)(2,1)S(1)}, bf16[1,8,64,128]{3,2,1,0:T(8,128)(2,1)}, u32[]{:S(2)}) copy-start(bf16[1,8,64,128]{3,2,1,0:T(8,128)(2,1)} %fields.1) | copy-start | bytes 393220
  4.2 0.9 %copy-start.3 = (bf16[1,8,64,128]{3,2,1,0:T(8,128)(2,1)S(1)}, bf16[1,8,64,128]{3,2,1,0:T(8,128)(2,1)}, u32[]{:S(2)}) copy-start(bf16[1,8,64,128]{3,2,1,0:T(8,128)(2,1)} %target.1) | copy-start | bytes 393220

commit v2 on v1

--- a/solution.py
+++ b/solution.py
@@ -23,15 +23,16 @@
 
 def kernel(
     nz, nb, lon, lat, ch, units,
+    fields_h, land_h, w_in_h, w_out_h, gain_h, offset_h, target_h,
+    output_h, grad_in_h, grad_out_h, gain_gradient_h, offset_gradient_h,
+    output, grad_in, grad_out, gain_gradient, offset_gradient,
     fields, land, w_in, w_out, gain, offset, target,
-    output, grad_in, grad_out, gain_gradient, offset_gradient,
     mask, first, dact, dpre, s_in, s_act, s_dout, w_back, dout_t,
-    rows1, head1, tail1, west1, east1,
-    rows2, head2, tail2, west2, east2,
+    rows1, rows2, heads, tails, wests, easts,
     stats1, stats2,
     part_a, pair_a, half_a, cross_a, mine_a, ring_a, full_a,
     part_b, pair_b, half_b, cross_b, mine_b, ring_b, full_b,
-    row_sems, col_sems, stat_sems, pair_sems, cross_sems, ring_sems, full_sems,
+    load_sems, store_sems, row_sems, col_sems, stat_sems, pair_sems, cross_sems, ring_sems, full_sems,
 ):
     nd = nz * nb
     nx = nb // 2
@@ -53,6 +54,11 @@
         )
 
     def over(count, fn):
+        if count <= 16:
+            for k in range(1, count):
+                fn(k)
+            return
+
         def step(k, carry):
             fn(k)
             return carry
@@ -77,10 +83,10 @@
     up = lax.rem(z + 1, nz)
     down = lax.rem(z + nz - 1, nz)
 
-    def col_copies(which, head, tail, west, east):
+    def col_copies(which):
         return (
-            copy(head, east, col_sems.at[which, 0, 0], col_sems.at[which, 1, 0], down, b),
-            copy(tail, west, col_sems.at[which, 0, 1], col_sems.at[which, 1, 1], up, b),
+            copy(heads.at[which], easts.at[which], col_sems.at[which, 0, 0], col_sems.at[which, 1, 0], down, b),
+            copy(tails.at[which], wests.at[which], col_sems.at[which, 0, 1], col_sems.at[which, 1, 1], up, b),
         )
 
     def stat_copy(which, buf, slot, peer):
@@ -99,6 +105,21 @@
     def drain_stats(which, buf):
         over(nd, lambda k: stat_copy(which, buf, me, lax.rem(me + k, nd)).wait_send())
 
+    loads = [
+        pltpu.make_async_copy(src, dst, load_sems.at[k])
+        for k, (src, dst) in enumerate((
+            (land_h, land), (fields_h, fields), (target_h, target), (w_in_h, w_in),
+            (w_out_h, w_out), (gain_h, gain), (offset_h, offset)))
+    ]
+    for load in loads:
+        load.start()
+    stores = [
+        pltpu.make_async_copy(src, dst, store_sems.at[k])
+        for k, (src, dst) in enumerate((
+            (output, output_h), (grad_in, grad_in_h), (grad_out, grad_out_h),
+            (gain_gradient, gain_gradient_h), (offset_gradient, offset_gradient_h)))
+    ]
+
     barrier = pltpu.get_barrier_semaphore()
 
     def greet(k):
@@ -110,6 +131,7 @@
     row_id = lax.broadcasted_iota(jnp.int32, (lat, ch), 0)
     zero_row = jnp.zeros((1, ch), F32)
 
+    loads[0].wait()
     land_f = land[...].astype(F32)
     diagonal = lax.broadcasted_iota(jnp.int32, (lat, lat), 0) == lax.broadcasted_iota(
         jnp.int32, (lat, lat), 1)
@@ -129,6 +151,8 @@
     def put(s, i, v, lane):
         s[i, :, lane * ch:(lane + 1) * ch] = v.astype(BF16)
 
+    loads[1].wait()
+    loads[2].wait()
     masked = [fields[0, i].astype(F32) * mask[at(i)] for i in range(lon)]
     seen = [target[0, i].astype(F32) * mask[at(i)] for i in range(lon)]
     halves = []
@@ -137,24 +161,48 @@
         halves.append(jnp.broadcast_to(jnp.sum(half, axis=0, keepdims=True), (8, ch)))
     rows1[z] = jnp.concatenate(
         [v[lat - 1:] for v in masked] + [v[lat - 1:] for v in seen] + halves, axis=0).astype(BF16)
-    head1[0:lat] = masked[0].astype(BF16)
-    head1[lat:2 * lat] = seen[0].astype(BF16)
-    tail1[0:lat] = masked[-1].astype(BF16)
-    tail1[lat:2 * lat] = seen[-1].astype(BF16)
-
+    for k, v in enumerate((masked, seen)):
+        heads[k] = v[0].astype(BF16)
+        tails[k] = v[-1].astype(BF16)
+
+    cols1 = col_copies(0)
+    cols_t = col_copies(1)
     pl.semaphore_wait(barrier, nd - 1)
+    for c in cols1:
+        c.start()
     send_rows(0, rows1)
-    cols1 = col_copies(0, head1, tail1, west1, east1)
-    for c in cols1:
+    for c in cols_t:
         c.start()
 
     for i in range(lon):
         put(s_in, i + 1, shift_down(masked[i]), 0)
         put(s_in, i + 1, masked[i], 1)
-    for tap in range(9):
-        f, s = tap // 3, tap % 3
-        w = w_out[f, s * ch:(s + 1) * ch, :].astype(F32)
-        w_back[f, s * ch:(s + 1) * ch, :] = w.T.astype(BF16)
+        put(s_in, i + 1, shift_up(masked[i], zero_row), 2)
+    for i in (0, lon + 1):
+        s_in[i] = jnp.zeros((lat, 3 * ch), BF16)
+
+    def window(s, f):
+        return s[f:f + lon].reshape(cells, 3 * ch)
+
+    def conv(s, w, order=(0, 1, 2)):
+        acc = jnp.dot(window(s, order[0]), w[0], preferred_element_type=F32)
+        acc += jnp.dot(window(s, order[1]), w[1], preferred_element_type=F32)
+        return acc + jnp.dot(window(s, order[2]), w[2], preferred_element_type=F32)
+
+    def fold_part(rows, w):
+        acc = jnp.zeros((2 * lon, ch), F32)
+        for f in range(3):
+            piece = jnp.concatenate(rows[f:f + lon] + [jnp.zeros((lon, ch), F32)], axis=0)
+            acc += jnp.dot(piece.astype(BF16), w[f, 2 * ch:3 * ch, :], preferred_element_type=F32)
+        return acc
+
+    def north(v, row):
+        return v + jnp.where(row_id == lat - 1, row, 0.0)
+
+    loads[3].wait()
+    first[...] = conv(s_in, w_in)
+    for load in loads[4:]:
+        load.wait()
 
     for c in cols1:
         c.wait_recv()
@@ -171,29 +219,34 @@
         return [left] + [facing[start + lon - 1 - i:start + lon - i] for i in range(lon)] + [right]
 
     ghost_in = ghosts(rows1, 0)
-    edge_w = west1[0:lat].astype(F32)
-    edge_e = east1[0:lat].astype(F32)
-    for i, v in ((0, edge_w), (lon + 1, edge_e)):
+    for i, v in ((0, wests[0].astype(F32)), (lon + 1, easts[0].astype(F32))):
         put(s_in, i, shift_down(v), 0)
         put(s_in, i, v, 1)
-    for i in range(lon + 2):
-        v = edge_w if i == 0 else edge_e if i == lon + 1 else (
-            fields[0, i - 1].astype(F32) * mask[at(i - 1)])
         put(s_in, i, shift_up(v, ghost_in[i]), 2)
-
-    def window(s, f):
-        return s[f:f + lon].reshape(cells, 3 * ch)
-
-    total = jnp.dot(window(s_in, 0), w_in[0], preferred_element_type=F32)
-    total += jnp.dot(window(s_in, 1), w_in[1], preferred_element_type=F32)
-    total += jnp.dot(window(s_in, 2), w_in[2], preferred_element_type=F32)
-    rounded = total.astype(BF16).astype(F32)
-    first[...] = rounded
-    held = rounded * mask[...]
-    stats1[me, 0:1] = jnp.sum(held, axis=0, keepdims=True)
-    stats1[me, 1:2] = jnp.sum(held * rounded, axis=0, keepdims=True)
+    from_west = jnp.dot(s_in[0], w_in[0], preferred_element_type=F32)
+    from_east = jnp.dot(s_in[lon + 1], w_in[2], preferred_element_type=F32)
+    extra = fold_part([zero_row] + ghost_in[1:lon + 1] + [zero_row], w_in)
+    sum_1 = jnp.zeros((lat, ch), F32)
+    sum_2 = jnp.zeros((lat, ch), F32)
+    for i in range(lon):
+        v = north(first[at(i)], extra[i:i + 1])
+        if i == 0:
+            v = v + from_west
+        if i == lon - 1:
+            v = v + from_east
+        v = v.astype(BF16).astype(F32)
+        first[at(i)] = v
+        held = v * mask[at(i)]
+        sum_1 += held
+        sum_2 += held * v
+    stats1[me, 0:1] = jnp.sum(sum_1, axis=0, keepdims=True)
+    stats1[me, 1:2] = jnp.sum(sum_2, axis=0, keepdims=True)
     send_stats(0, stats1)
 
+    for tap in range(9):
+        f, t = tap // 3, tap % 3
+        w = w_out[f, t * ch:(t + 1) * ch, :].astype(F32)
+        w_back[f, t * ch:(t + 1) * ch, :] = w.T.astype(BF16)
     count = zero_row
     for k in range(nz):
         packet = rows1[k].astype(F32)
@@ -204,11 +257,13 @@
     def scaled(v):
         return (v * scale).astype(BF16).astype(F32)
 
+    for c in cols_t:
+        c.wait_recv()
     for i in range(lon + 2):
         if i == 0:
-            v = west1[lat:2 * lat].astype(F32)
+            v = wests[1].astype(F32)
         elif i == lon + 1:
-            v = east1[lat:2 * lat].astype(F32)
+            v = easts[1].astype(F32)
         else:
             v = target[0, i - 1].astype(F32) * mask[at(i - 1)]
         v = scaled(v)
@@ -220,16 +275,13 @@
             dout_t[:, (i - 2) * lat:i * lat] = pair.T.astype(BF16)
         earlier = v
     ghost_dout = [scaled(v) for v in ghosts(rows1, lon)]
-    total = jnp.dot(window(s_dout, 2), w_back[0], preferred_element_type=F32)
-    total += jnp.dot(window(s_dout, 1), w_back[1], preferred_element_type=F32)
-    total += jnp.dot(window(s_dout, 0), w_back[2], preferred_element_type=F32)
-    extra = jnp.zeros((2 * lon, ch), F32)
-    for f in range(3):
-        piece = jnp.concatenate(ghost_dout[f:f + lon] + [jnp.zeros((lon, ch), F32)], axis=0)
-        extra += jnp.dot(piece.astype(BF16), w_back[f, 2 * ch:3 * ch, :], preferred_element_type=F32)
+    total = conv(s_dout, w_back, (2, 1, 0))
+    extra = fold_part(ghost_dout, w_back)
     for i in range(lon):
-        dact[at(i)] = total[i * lat:(i + 1) * lat] + jnp.where(
-            row_id == lat - 1, extra[i:i + 1], 0.0)
+        dact[at(i)] = north(total[i * lat:(i + 1) * lat], extra[i:i + 1])
+    for i in range(lon):
+        v = s_in[i + 1, :, ch:2 * ch].astype(F32)
+        put(s_in, i + 1, shift_up(v, ghost_in[i + 1]), 2)
 
     recv_stats(0, stats1)
 
@@ -260,14 +312,14 @@
         s_act[i + 1, :, ch:2 * ch] = act
         last.append(act.astype(F32)[lat - 1:])
         if i == 0:
-            head2[...] = act
+            heads[2] = act
         if i == lon - 1:
-            tail2[...] = act
+            tails[2] = act
     stats2[me, 0:1] = sum_off
     stats2[me, 1:2] = sum_gain
     send_stats(1, stats2)
     rows2[z] = jnp.concatenate(last + [jnp.zeros((lon, ch), F32)], axis=0).astype(BF16)
-    cols2 = col_copies(1, head2, tail2, west2, east2)
+    cols2 = col_copies(2)
     for c in cols2:
         c.start()
     send_rows(1, rows2)
@@ -278,8 +330,8 @@
         c.wait_recv()
     recv_rows(1, rows2)
     ghost_act = ghosts(rows2, 0)
-    s_act[0, :, ch:2 * ch] = west2[...]
-    s_act[lon + 1, :, ch:2 * ch] = east2[...]
+    s_act[0, :, ch:2 * ch] = wests[2]
+    s_act[lon + 1, :, ch:2 * ch] = easts[2]
     for i in range(lon + 2):
         v = s_act[i, :, ch:2 * ch].astype(F32)
         if i == 0 or i == lon + 1:
@@ -290,7 +342,10 @@
     live = 9 * share
     padded = units * 16 * nz
 
-    def tap_grad(s, d_t, part):
+    def rows_of(f):
+        return pl.ds(3 * f * share, 3 * share)
+
+    def tap_grad(which, s, d_t, part, pair):
         for f in range(3):
             g = jnp.dot(d_t, window(s, f), preferred_element_type=F32).astype(BF16)
             for t in range(3):
@@ -298,17 +353,16 @@
                 for k in range(nb):
                     part[k % 2, k // 2, tap * share:(tap + 1) * share, :] = (
                         g[k * share:(k + 1) * share, t * ch:(t + 1) * ch])
-        if padded > live:
-            for k in range(nb):
-                part[k % 2, k // 2, live:padded, :] = jnp.zeros((padded - live, ch), BF16)
-
-    def pair_copy(which, part, pair):
-        return copy(part.at[other], pair, pair_sems.at[which, 0], pair_sems.at[which, 1],
-                    z, 2 * col + other)
-
-    def cross_copy(which, half, cross, slot, peer, x):
-        return copy(half.at[peer], cross.at[slot], cross_sems.at[which, 0, peer],
-                    cross_sems.at[which, 1, slot], z, 2 * x + core)
+            pair_copy(which, f, part, pair).start()
+
+    def pair_copy(which, f, part, pair):
+        return copy(part.at[other, :, rows_of(f)], pair.at[:, rows_of(f)],
+                    pair_sems.at[which, 0, f], pair_sems.at[which, 1, f], z, 2 * col + other)
+
+    def cross_copy(which, f, half, cross, slot, peer, x):
+        return copy(half.at[peer, rows_of(f)], cross.at[slot, rows_of(f)],
+                    cross_sems.at[which, 0, f, peer], cross_sems.at[which, 1, f, slot],
+                    z, 2 * x + core)
 
     def ring_copy(which, mine, ring, slot, peer):
         return copy(mine.at[peer], ring.at[slot], ring_sems.at[which, 0, peer],
@@ -319,21 +373,27 @@
                     full_sems.at[which, 1, slot], peer, b)
 
     def after_pair(which, part, pair, half, cross):
-        pair_copy(which, part, pair).wait_recv()
-        for x in range(nx):
-            half[x] = (part[core, x].astype(F32) + pair[x].astype(F32)).astype(BF16)
-
-        def one(k):
-            x = lax.rem(col + k, nx)
-            cross_copy(which, half, cross, col, x, x).start()
-        over(nx, one)
+        for f in range(3):
+            pair_copy(which, f, part, pair).wait_recv()
+            for x in range(nx):
+                half[x, rows_of(f)] = (
+                    part[core, x, rows_of(f)].astype(F32) + pair[x, rows_of(f)].astype(F32)
+                ).astype(BF16)
+
+            def one(k):
+                x = lax.rem(col + k, nx)
+                cross_copy(which, f, half, cross, col, x, x).start()
+            over(nx, one)
 
     def after_cross(which, half, cross, mine, ring):
         acc = half[col].astype(F32)
         for k in range(1, nx):
             x = lax.rem(col + k, nx)
-            cross_copy(which, half, cross, x, x, x).wait_recv()
+            for f in range(3):
+                cross_copy(which, f, half, cross, x, x, x).wait_recv()
             acc = acc + cross[x].astype(F32)
+        if padded > live:
+            acc = jnp.concatenate([acc, jnp.zeros((padded - live, ch), F32)], axis=0)
         for k in range(nz):
             mine[k] = acc[k * units * 16:(k + 1) * units * 16].astype(BF16)
 
@@ -362,12 +422,13 @@
         out[...] = full[...].reshape(padded, ch)[0:live].astype(F32)
 
     def drain(which, part, pair, half, cross, mine, ring, full):
-        pair_copy(which, part, pair).wait_send()
-
-        def one_x(k):
-            x = lax.rem(col + k, nx)
-            cross_copy(which, half, cross, col, x, x).wait_send()
-        over(nx, one_x)
+        for f in range(3):
+            pair_copy(which, f, part, pair).wait_send()
+
+            def one_x(k):
+                x = lax.rem(col + k, nx)
+                cross_copy(which, f, half, cross, col, x, x).wait_send()
+            over(nx, one_x)
 
         def one_z(k):
             peer = lax.rem(z + k, nz)
@@ -375,8 +436,7 @@
             full_copy(which, full, z, peer).wait_send()
         over(nz, one_z)
 
-    tap_grad(s_act, dout_t[...], part_a)
-    pair_copy(0, part_a, pair_a).start()
+    tap_grad(0, s_act, dout_t[...], part_a, pair_a)
 
     recv_stats(1, stats2)
     acc = gathered(stats2)
@@ -384,6 +444,8 @@
     gain_total = acc[1:2]
     offset_gradient[...] = off_total
     gain_gradient[...] = gain_total
+    stores[3].start()
+    stores[4].start()
     for i in range(0, lon, 2):
         pieces = []
         for j in (i, i + 1):
@@ -392,25 +454,24 @@
                 dpre[at(j)] - (off_total + xhat * gain_total) / count))
         pair = jnp.concatenate(pieces, axis=0)
         dout_t[:, i * lat:(i + 2) * lat] = pair.T.astype(BF16)
-    tap_grad(s_in, dout_t[...], part_b)
-    pair_copy(1, part_b, pair_b).start()
-
     after_pair(0, part_a, pair_a, half_a, cross_a)
+    tap_grad(1, s_in, dout_t[...], part_b, pair_b)
+    after_cross(0, half_a, cross_a, mine_a, ring_a)
     after_pair(1, part_b, pair_b, half_b, cross_b)
 
-    total = jnp.dot(window(s_act, 0), w_out[0], preferred_element_type=F32)
-    total += jnp.dot(window(s_act, 1), w_out[1], preferred_element_type=F32)
-    total += jnp.dot(window(s_act, 2), w_out[2], preferred_element_type=F32)
+    total = conv(s_act, w_out)
     output[0] = (total * mask[...]).astype(BF16).reshape(lon, lat, ch)
-
-    after_cross(0, half_a, cross_a, mine_a, ring_a)
+    stores[0].start()
+
+    after_ring(0, mine_a, ring_a, full_a)
     after_cross(1, half_b, cross_b, mine_b, ring_b)
-    after_ring(0, mine_a, ring_a, full_a)
     after_ring(1, mine_b, ring_b, full_b)
     after_full(0, full_a, grad_out)
+    stores[2].start()
     after_full(1, full_b, grad_in)
-
-    for c in cols1 + cols2:
+    stores[1].start()
+
+    for c in cols1 + cols_t + cols2:
         c.wait_send()
     drain_rows(0, rows1)
     drain_rows(1, rows2)
@@ -418,6 +479,17 @@
     drain_stats(1, stats2)
     drain(0, part_a, pair_a, half_a, cross_a, mine_a, ring_a, full_a)
     drain(1, part_b, pair_b, half_b, cross_b, mine_b, ring_b, full_b)
+    for store in stores:
+        store.wait()
+
+
+def writer(*refs):
+    sems = refs[-1]
+    copies = [pltpu.make_async_copy(refs[k], refs[5 + k], sems.at[k]) for k in range(5)]
+    for c in copies:
+        c.start()
+    for c in copies:
+        c.wait()
 
 
 def body(nz, nb, fields, land, conv_in, conv_out, gain, offset, target):
@@ -429,16 +501,28 @@
     padded = units * 16 * nz
     vm = pltpu.VMEM
     reduction = [
-        vm((2, nx, padded, ch), BF16),
-        vm((nx, padded, ch), BF16),
-        vm((nx, padded, ch), BF16),
-        vm((nx, padded, ch), BF16),
+        vm((2, nx, 9 * share, ch), BF16),
+        vm((nx, 9 * share, ch), BF16),
+        vm((nx, 9 * share, ch), BF16),
+        vm((nx, 9 * share, ch), BF16),
         vm((nz, units * 16, ch), BF16),
         vm((nz, units * 16, ch), BF16),
         vm((nz, units * 16, ch), BF16),
     ]
     dma = pltpu.SemaphoreType.DMA
     scratch = [
+        vm(fields.shape, BF16),
+        vm((9 * share, ch), F32),
+        vm((9 * share, ch), F32),
+        vm((1, ch), F32),
+        vm((1, ch), F32),
+        vm(fields.shape, BF16),
+        vm(land.shape, jnp.int32),
+        vm((3, 3 * ch, ch), BF16),
+        vm((3, 3 * ch, ch), BF16),
+        vm((1, ch), F32),
+        vm((1, ch), F32),
+        vm(target.shape, BF16),
         vm((lon * lat, ch), F32),
         vm((lon * lat, ch), F32),
         vm((lon * lat, ch), F32),
@@ -449,25 +533,26 @@
         vm((3, 3 * ch, ch), BF16),
         vm((ch, lon * lat), BF16),
         vm((nz, 32, ch), BF16),
-        vm((2 * lat, ch), BF16), vm((2 * lat, ch), BF16),
-        vm((2 * lat, ch), BF16), vm((2 * lat, ch), BF16),
         vm((nz, 16, ch), BF16),
-        vm((lat, ch), BF16), vm((lat, ch), BF16),
-        vm((lat, ch), BF16), vm((lat, ch), BF16),
-        vm((nd, 8, ch), F32),
-        vm((nd, 8, ch), F32),
+        vm((3, lat, ch), BF16), vm((3, lat, ch), BF16),
+        vm((3, lat, ch), BF16), vm((3, lat, ch), BF16),
+        vm((nd, 2, ch), F32),
+        vm((nd, 2, ch), F32),
         *reduction,
         *reduction,
+        dma((7,)),
+        dma((5,)),
         dma((2, 2, nz)),
-        dma((2, 2, 2)),
+        dma((3, 2, 2)),
         dma((2, 2, nd)),
-        dma((2, 2)),
-        dma((2, 2, nx)),
+        dma((2, 2, 3)),
+        dma((2, 2, 3, nx)),
         dma((2, 2, nz)),
         dma((2, 2, nz)),
     ]
-    spec = pl.BlockSpec(memory_space=pltpu.VMEM)
-    out, grad_in, grad_out, gain_gradient, offset_gradient = pl.pallas_call(
+    anywhere = pl.BlockSpec(memory_space=pl.ANY)
+    limit = 62 * 1024 * 1024
+    results = pl.pallas_call(
         functools.partial(kernel, nz, nb, lon, lat, ch, units),
         out_shape=(
             jax.ShapeDtypeStruct(fields.shape, BF16),
@@ -476,17 +561,26 @@
             jax.ShapeDtypeStruct((1, ch), F32),
             jax.ShapeDtypeStruct((1, ch), F32),
         ),
-        in_specs=[spec] * 7,
-        out_specs=(spec,) * 5,
+        in_specs=[anywhere] * 7,
+        out_specs=(anywhere,) * 5,
         scratch_shapes=scratch,
         compiler_params=pltpu.CompilerParams(
-            collective_id=0, has_side_effects=True, vmem_limit_bytes=40 * 1024 * 1024
+            collective_id=0, has_side_effects=True, vmem_limit_bytes=limit
         ),
     )(
         fields, land,
         conv_in.reshape(3, 3 * ch, ch), conv_out.reshape(3, 3 * ch, ch),
         gain.reshape(1, ch), offset.reshape(1, ch), target,
     )
+
+    out, grad_in, grad_out, gain_gradient, offset_gradient = pl.pallas_call(
+        writer,
+        out_shape=tuple(jax.ShapeDtypeStruct(r.shape, r.dtype) for r in results),
+        in_specs=[anywhere] * 5,
+        out_specs=(anywhere,) * 5,
+        scratch_shapes=[dma((5,))],
+        compiler_params=pltpu.CompilerParams(vmem_limit_bytes=limit),
+    )(*results)
 
     def taps(g):
         return g.reshape(9, share, ch).transpose(0, 2, 1)

time: 45 us -> 53.7 us (1.19)
  Pallas kernels: 36.6 us -> 52.8 us
  local copies, waits for them, and re-layouts: 7.4 us -> 0 us
    pallas_call x0 -> x1, Pallas kernels: none -> 14.1 us  [body(): pl.pallas_call(writer, out_shape=tuple((jax.ShapeDtypeStruct(r.shape, r.d...]
    unnamed x19 -> x0, local copies, waits for them, and re-layouts: 7.4 us -> none
    pallas_call x1, Pallas kernels: 36.6 us -> 38.7 us  [body(): pl.pallas_call(functools.partial(kernel, nz, nb, lon, lat, ch, units), ou...]
where the time goes in v2:
time: 53.7 us; the launch traced here: 53.5 us
  Pallas kernels  52.8 us (98%)
  between operations  0.64 us (1%)
    pallas_call x1, Pallas kernels, body(): pl.pallas_call(functools.partial(kernel, nz, nb, lon, lat, ch, units), ou...  38.7 us
    pallas_call x1, Pallas kernels, body(): pl.pallas_call(writer, out_shape=tuple((jax.ShapeDtypeStruct(r.shape, r.d...  14.1 us

profile of v2, /device:TPU:0, one launch (start us, length us, event | category | flops | bytes accessed | tf_op | source)
XLA Modules:
  0.0 53.5 jit_solution(13902667421972692367)
XLA Ops:
  0.6 38.7 %shard_map.110 = (bf16[1,8,64,128]{3,2,1,0:T(8,128)(2,1)}, f32[288,128]{1,0:T(8,128)}, f32[288,128]{1,0:T(8,128)}, f32[1,128]{1,0:T(1,128)}, f32[1,128]{1,0:T(1,128)}) custom-call(bf16[1,8,64,128]{3,2,1,0:T(8,128)(2,1)} %fields_h.1, s32[8,64]{1,0:T(8,128)} %land_h.1, bf16[3,384,128]{2,1,0:T(8,128)(2,1)} %bitcast.12, bf16[3,384,128]{2,1,0:T(8,128)(2,1)} %bitcast.13, ...), custom_call_target="tpu_custom_call" | custom-call | tf_op jit(solution)/shard_map/pallas_call | solution.py:555
  39.4 14.1 %shard_map.111 = (bf16[1,8,64,128]{3,2,1,0:T(8,128)(2,1)}, f32[288,128]{1,0:T(8,128)}, f32[288,128]{1,0:T(8,128)}, f32[1,128]{1,0:T(1,128)}, f32[1,128]{1,0:T(1,128)}) custom-call(bf16[1,8,64,128]{3,2,1,0:T(8,128)(2,1)} %get-tuple-element.15.refs_0_, f32[288,128]{1,0:T(8,128)} %get-tuple-element.16.refs_1_, f32[288,128]{1,0:T(8,128)} %get-tuple-element.17.refs_2_, ...), custom_call_target="tpu_custom_call" | custom-call | tf_op jit(solution)/shard_map/pallas_call | solution.py:576

commit v3 on v2

--- a/solution.py
+++ b/solution.py
@@ -29,17 +29,15 @@
     fields, land, w_in, w_out, gain, offset, target,
     mask, first, dact, dpre, s_in, s_act, s_dout, w_back, dout_t,
     rows1, rows2, heads, tails, wests, easts,
-    stats1, stats2,
+    by_batch, by_space,
     part_a, pair_a, half_a, cross_a, mine_a, ring_a, full_a,
     part_b, pair_b, half_b, cross_b, mine_b, ring_b, full_b,
-    load_sems, store_sems, row_sems, col_sems, stat_sems, pair_sems, cross_sems, ring_sems, full_sems,
+    load_sems, store_sems, row_sems, col_sems, batch_sems, space_sems, pair_sems, cross_sems, ring_sems, full_sems,
 ):
-    nd = nz * nb
     nx = nb // 2
     cells = lon * lat
     z = lax.axis_index("space")
     b = lax.axis_index("batch")
-    me = z * nb + b
     core = lax.rem(b, 2)
     col = b // 2
     other = 1 - core
@@ -89,21 +87,40 @@
             copy(tails.at[which], wests.at[which], col_sems.at[which, 0, 1], col_sems.at[which, 1, 1], up, b),
         )
 
-    def stat_copy(which, buf, slot, peer):
-        return copy(buf.at[slot], buf.at[slot], stat_sems.at[which, 0, peer],
-                    stat_sems.at[which, 1, slot], peer // nb, lax.rem(peer, nb))
-
-    def send_stats(which, buf):
-        over(nd, lambda k: stat_copy(which, buf, me, lax.rem(me + k, nd)).start())
-
-    def recv_stats(which, buf):
-        def one(k):
-            src = lax.rem(me + k, nd)
-            stat_copy(which, buf, src, src).wait_recv()
-        over(nd, one)
-
-    def drain_stats(which, buf):
-        over(nd, lambda k: stat_copy(which, buf, me, lax.rem(me + k, nd)).wait_send())
+    def batch_copy(which, slot, peer):
+        return copy(by_batch.at[which, slot], by_batch.at[which, slot],
+                    batch_sems.at[which, 0, peer], batch_sems.at[which, 1, slot], z, peer)
+
+    def space_copy(which, slot, peer):
+        return copy(by_space.at[which, slot], by_space.at[which, slot],
+                    space_sems.at[which, 0, peer], space_sems.at[which, 1, slot], peer, b)
+
+    def send_stats(which):
+        over(nb, lambda k: batch_copy(which, b, lax.rem(b + k, nb)).start())
+
+    def recv_stats(which):
+        def one_b(k):
+            src = lax.rem(b + k, nb)
+            batch_copy(which, src, src).wait_recv()
+        over(nb, one_b)
+        acc = by_batch[which, 0]
+        for k in range(1, nb):
+            acc = acc + by_batch[which, k]
+        by_space[which, z] = acc
+        over(nz, lambda k: space_copy(which, z, lax.rem(z + k, nz)).start())
+
+        def one_z(k):
+            src = lax.rem(z + k, nz)
+            space_copy(which, src, src).wait_recv()
+        over(nz, one_z)
+        acc = by_space[which, 0]
+        for k in range(1, nz):
+            acc = acc + by_space[which, k]
+        return acc
+
+    def drain_stats(which):
+        over(nb, lambda k: batch_copy(which, b, lax.rem(b + k, nb)).wait_send())
+        over(nz, lambda k: space_copy(which, z, lax.rem(z + k, nz)).wait_send())
 
     loads = [
         pltpu.make_async_copy(src, dst, load_sems.at[k])
@@ -122,11 +139,11 @@
 
     barrier = pltpu.get_barrier_semaphore()
 
-    def greet(k):
-        peer = lax.rem(me + k, nd)
-        pl.semaphore_signal(barrier, inc=1, device_id=device(peer // nb, lax.rem(peer, nb)),
+    def greet(zz, bb):
+        pl.semaphore_signal(barrier, inc=1, device_id=device(zz, bb),
                             device_id_type=pl.DeviceIdType.MESH)
-    over(nd, greet)
+    over(nz, lambda k: greet(lax.rem(z + k, nz), b))
+    over(nb, lambda k: greet(z, lax.rem(b + k, nb)))
 
     row_id = lax.broadcasted_iota(jnp.int32, (lat, ch), 0)
     zero_row = jnp.zeros((1, ch), F32)
@@ -167,7 +184,7 @@
 
     cols1 = col_copies(0)
     cols_t = col_copies(1)
-    pl.semaphore_wait(barrier, nd - 1)
+    pl.semaphore_wait(barrier, nz + nb - 2)
     for c in cols1:
         c.start()
     send_rows(0, rows1)
@@ -239,9 +256,9 @@
         held = v * mask[at(i)]
         sum_1 += held
         sum_2 += held * v
-    stats1[me, 0:1] = jnp.sum(sum_1, axis=0, keepdims=True)
-    stats1[me, 1:2] = jnp.sum(sum_2, axis=0, keepdims=True)
-    send_stats(0, stats1)
+    by_batch[0, b, 0:1] = jnp.sum(sum_1, axis=0, keepdims=True)
+    by_batch[0, b, 1:2] = jnp.sum(sum_2, axis=0, keepdims=True)
+    send_stats(0)
 
     for tap in range(9):
         f, t = tap // 3, tap % 3
@@ -283,15 +300,7 @@
         v = s_in[i + 1, :, ch:2 * ch].astype(F32)
         put(s_in, i + 1, shift_up(v, ghost_in[i + 1]), 2)
 
-    recv_stats(0, stats1)
-
-    def gathered(buf):
-        acc = buf[0]
-        for k in range(1, nd):
-            acc = acc + buf[k]
-        return acc
-
-    acc = gathered(stats1)
+    acc = recv_stats(0)
     mean = acc[0:1] / count
     var = acc[1:2] / count - mean * mean
     inverse = lax.rsqrt(var + 1e-05)
@@ -315,9 +324,9 @@
             heads[2] = act
         if i == lon - 1:
             tails[2] = act
-    stats2[me, 0:1] = sum_off
-    stats2[me, 1:2] = sum_gain
-    send_stats(1, stats2)
+    by_batch[1, b, 0:1] = sum_off
+    by_batch[1, b, 1:2] = sum_gain
+    send_stats(1)
     rows2[z] = jnp.concatenate(last + [jnp.zeros((lon, ch), F32)], axis=0).astype(BF16)
     cols2 = col_copies(2)
     for c in cols2:
@@ -438,8 +447,7 @@
 
     tap_grad(0, s_act, dout_t[...], part_a, pair_a)
 
-    recv_stats(1, stats2)
-    acc = gathered(stats2)
+    acc = recv_stats(1)
     off_total = acc[0:1]
     gain_total = acc[1:2]
     offset_gradient[...] = off_total
@@ -475,8 +483,8 @@
         c.wait_send()
     drain_rows(0, rows1)
     drain_rows(1, rows2)
-    drain_stats(0, stats1)
-    drain_stats(1, stats2)
+    drain_stats(0)
+    drain_stats(1)
     drain(0, part_a, pair_a, half_a, cross_a, mine_a, ring_a, full_a)
     drain(1, part_b, pair_b, half_b, cross_b, mine_b, ring_b, full_b)
     for store in stores:
@@ -484,17 +492,20 @@
 
 
 def writer(*refs):
-    sems = refs[-1]
-    copies = [pltpu.make_async_copy(refs[k], refs[5 + k], sems.at[k]) for k in range(5)]
-    for c in copies:
+    sources, results, held, sems = refs[:5], refs[5:10], refs[10:15], refs[15]
+    loads = [pltpu.make_async_copy(sources[k], held[k], sems.at[0, k]) for k in range(5)]
+    stores = [pltpu.make_async_copy(held[k], results[k], sems.at[1, k]) for k in range(5)]
+    for c in loads:
         c.start()
-    for c in copies:
+    for load, store in zip(loads, stores):
+        load.wait()
+        store.start()
+    for c in stores:
         c.wait()
 
 
 def body(nz, nb, fields, land, conv_in, conv_out, gain, offset, target):
     lon, lat, ch = fields.shape[1:]
-    nd = nz * nb
     nx = nb // 2
     share = ch // nb
     units = -(-(9 * share // 16) // nz)
@@ -536,15 +547,16 @@
         vm((nz, 16, ch), BF16),
         vm((3, lat, ch), BF16), vm((3, lat, ch), BF16),
         vm((3, lat, ch), BF16), vm((3, lat, ch), BF16),
-        vm((nd, 2, ch), F32),
-        vm((nd, 2, ch), F32),
+        vm((2, nb, 2, ch), F32),
+        vm((2, nz, 2, ch), F32),
         *reduction,
         *reduction,
         dma((7,)),
         dma((5,)),
         dma((2, 2, nz)),
         dma((3, 2, 2)),
-        dma((2, 2, nd)),
+        dma((2, 2, nb)),
+        dma((2, 2, nz)),
         dma((2, 2, 3)),
         dma((2, 2, 3, nx)),
         dma((2, 2, nz)),
@@ -578,7 +590,7 @@
         out_shape=tuple(jax.ShapeDtypeStruct(r.shape, r.dtype) for r in results),
         in_specs=[anywhere] * 5,
         out_specs=(anywhere,) * 5,
-        scratch_shapes=[dma((5,))],
+        scratch_shapes=[vm(r.shape, r.dtype) for r in results] + [dma((2, 5))],
         compiler_params=pltpu.CompilerParams(vmem_limit_bytes=limit),
     )(*results)
 

time: 53.7 us -> 44.6 us (0.83)
  Pallas kernels: 52.8 us -> 43.8 us
    pallas_call x1, Pallas kernels: 14.1 us -> 1.8 us  [body(): pl.pallas_call(writer, out_shape=tuple((jax.ShapeDtypeStruct(r.shape, r.d...]
    pallas_call x1, Pallas kernels: 38.7 us -> 42 us  [body(): pl.pallas_call(functools.partial(kernel, nz, nb, lon, lat, ch, units), ou...]
where the time goes in v3:
time: 44.6 us; the launch traced here: 44.4 us
  Pallas kernels  43.8 us (98%)
  between operations  0.64 us (1%)
    pallas_call x1, Pallas kernels, body(): pl.pallas_call(functools.partial(kernel, nz, nb, lon, lat, ch, units), ou...  42 us
    pallas_call x1, Pallas kernels, body(): pl.pallas_call(writer, out_shape=tuple((jax.ShapeDtypeStruct(r.shape, r.d...  1.8 us

profile of v3, /device:TPU:0, one launch (start us, length us, event | category | flops | bytes accessed | tf_op | source)
XLA Modules:
  0.0 44.4 jit_solution(14023191212598763035)
XLA Ops:
  0.6 42.0 %shard_map.110 = (bf16[1,8,64,128]{3,2,1,0:T(8,128)(2,1)}, f32[288,128]{1,0:T(8,128)}, f32[288,128]{1,0:T(8,128)}, f32[1,128]{1,0:T(1,128)}, f32[1,128]{1,0:T(1,128)}) custom-call(bf16[1,8,64,128]{3,2,1,0:T(8,128)(2,1)} %fields_h.1, s32[8,64]{1,0:T(8,128)} %land_h.1, bf16[3,384,128]{2,1,0:T(8,128)(2,1)} %bitcast.12, bf16[3,384,128]{2,1,0:T(8,128)(2,1)} %bitcast.13, ...), custom_call_target="tpu_custom_call" | custom-call | tf_op jit(solution)/shard_map/pallas_call | solution.py:567
  42.6 1.8 %shard_map.111 = (bf16[1,8,64,128]{3,2,1,0:T(8,128)(2,1)}, f32[288,128]{1,0:T(8,128)}, f32[288,128]{1,0:T(8,128)}, f32[1,128]{1,0:T(1,128)}, f32[1,128]{1,0:T(1,128)}) custom-call(bf16[1,8,64,128]{3,2,1,0:T(8,128)(2,1)} %get-tuple-element.15.refs_0_, f32[288,128]{1,0:T(8,128)} %get-tuple-element.16.refs_1_, f32[288,128]{1,0:T(8,128)} %get-tuple-element.17.refs_2_, ...), custom_call_target="tpu_custom_call" | custom-call | tf_op jit(solution)/shard_map/pallas_call | solution.py:588

commit v4 on v2

--- a/solution.py
+++ b/solution.py
@@ -29,7 +29,7 @@
     fields, land, w_in, w_out, gain, offset, target,
     mask, first, dact, dpre, s_in, s_act, s_dout, w_back, dout_t,
     rows1, rows2, heads, tails, wests, easts,
-    stats1, stats2,
+    stats, ghost_f, ghost_d, ghost_a, fold,
     part_a, pair_a, half_a, cross_a, mine_a, ring_a, full_a,
     part_b, pair_b, half_b, cross_b, mine_b, ring_b, full_b,
     load_sems, store_sems, row_sems, col_sems, stat_sems, pair_sems, cross_sems, ring_sems, full_sems,
@@ -54,7 +54,7 @@
         )
 
     def over(count, fn):
-        if count <= 16:
+        if count <= 4:
             for k in range(1, count):
                 fn(k)
             return
@@ -89,21 +89,25 @@
             copy(tails.at[which], wests.at[which], col_sems.at[which, 0, 1], col_sems.at[which, 1, 1], up, b),
         )
 
-    def stat_copy(which, buf, slot, peer):
-        return copy(buf.at[slot], buf.at[slot], stat_sems.at[which, 0, peer],
+    def stat_copy(which, slot, peer):
+        return copy(stats.at[which, slot], stats.at[which, slot], stat_sems.at[which, 0, peer],
                     stat_sems.at[which, 1, slot], peer // nb, lax.rem(peer, nb))
 
-    def send_stats(which, buf):
-        over(nd, lambda k: stat_copy(which, buf, me, lax.rem(me + k, nd)).start())
-
-    def recv_stats(which, buf):
+    def send_stats(which):
+        over(nd, lambda k: stat_copy(which, me, lax.rem(me + k, nd)).start())
+
+    def recv_stats(which):
         def one(k):
             src = lax.rem(me + k, nd)
-            stat_copy(which, buf, src, src).wait_recv()
+            stat_copy(which, src, src).wait_recv()
         over(nd, one)
-
-    def drain_stats(which, buf):
-        over(nd, lambda k: stat_copy(which, buf, me, lax.rem(me + k, nd)).wait_send())
+        acc = stats[which, 0]
+        for k in range(1, nd):
+            acc = acc + stats[which, k]
+        return acc
+
+    def drain_stats(which):
+        over(nd, lambda k: stat_copy(which, me, lax.rem(me + k, nd)).wait_send())
 
     loads = [
         pltpu.make_async_copy(src, dst, load_sems.at[k])
@@ -140,7 +144,13 @@
     mask[...] = jnp.dot(spread.astype(BF16), jnp.ones((lat, ch), BF16), preferred_element_type=F32)
 
     def at(i):
-        return pl.ds(i * lat, lat)
+        return pl.ds(pl.multiple_of(i * lat, lat), lat)
+
+    def loop(start, stop, fn):
+        def step(i, carry):
+            fn(i)
+            return carry
+        lax.fori_loop(start, stop, step, 0)
 
     def shift_up(v, ghost):
         return jnp.concatenate([v[1:], ghost], axis=0)
@@ -153,17 +163,28 @@
 
     loads[1].wait()
     loads[2].wait()
-    masked = [fields[0, i].astype(F32) * mask[at(i)] for i in range(lon)]
-    seen = [target[0, i].astype(F32) * mask[at(i)] for i in range(lon)]
+    def base(s, i, v):
+        put(s, i, shift_down(v), 0)
+        put(s, i, v, 1)
+        put(s, i, shift_up(v, zero_row), 2)
+
+    def mask_lon(i):
+        base(s_in, i + 1, fields[0, i].astype(F32) * mask[at(i)])
+        target[0, i] = (target[0, i].astype(F32) * mask[at(i)]).astype(BF16)
+    loop(0, lon, mask_lon)
+
     halves = []
     for h in range(2):
         half = mask[h * cells // 2:(h + 1) * cells // 2]
         halves.append(jnp.broadcast_to(jnp.sum(half, axis=0, keepdims=True), (8, ch)))
     rows1[z] = jnp.concatenate(
-        [v[lat - 1:] for v in masked] + [v[lat - 1:] for v in seen] + halves, axis=0).astype(BF16)
-    for k, v in enumerate((masked, seen)):
-        heads[k] = v[0].astype(BF16)
-        tails[k] = v[-1].astype(BF16)
+        [s_in[i + 1, lat - 16:, ch:2 * ch].astype(F32)[15:] for i in range(lon)]
+        + [target[0, i, lat - 16:].astype(F32)[15:] for i in range(lon)] + halves, axis=0
+    ).astype(BF16)
+    heads[0] = s_in[1, :, ch:2 * ch]
+    tails[0] = s_in[lon, :, ch:2 * ch]
+    heads[1] = target[0, 0]
+    tails[1] = target[0, lon - 1]
 
     cols1 = col_copies(0)
     cols_t = col_copies(1)
@@ -174,20 +195,22 @@
     for c in cols_t:
         c.start()
 
-    for i in range(lon):
-        put(s_in, i + 1, shift_down(masked[i]), 0)
-        put(s_in, i + 1, masked[i], 1)
-        put(s_in, i + 1, shift_up(masked[i], zero_row), 2)
     for i in (0, lon + 1):
         s_in[i] = jnp.zeros((lat, 3 * ch), BF16)
 
     def window(s, f):
-        return s[f:f + lon].reshape(cells, 3 * ch)
-
-    def conv(s, w, order=(0, 1, 2)):
-        acc = jnp.dot(window(s, order[0]), w[0], preferred_element_type=F32)
-        acc += jnp.dot(window(s, order[1]), w[1], preferred_element_type=F32)
-        return acc + jnp.dot(window(s, order[2]), w[2], preferred_element_type=F32)
+        return s[pl.ds(f, lon)].reshape(cells, 3 * ch)
+
+    def conv(s, w, out, order=(0, 1, 2)):
+        part_lon = lon // 2
+
+        def half(h):
+            acc = jnp.zeros((part_lon * lat, ch), F32)
+            for f in range(3):
+                piece = s[pl.ds(h * part_lon + order[f], part_lon)].reshape(part_lon * lat, 3 * ch)
+                acc += jnp.dot(piece, w[f], preferred_element_type=F32)
+            out[pl.ds(pl.multiple_of(h * part_lon * lat, part_lon * lat), part_lon * lat)] = acc
+        loop(0, 2, half)
 
     def fold_part(rows, w):
         acc = jnp.zeros((2 * lon, ch), F32)
@@ -200,7 +223,7 @@
         return v + jnp.where(row_id == lat - 1, row, 0.0)
 
     loads[3].wait()
-    first[...] = conv(s_in, w_in)
+    conv(s_in, w_in, first)
     for load in loads[4:]:
         load.wait()
 
@@ -225,28 +248,30 @@
         put(s_in, i, shift_up(v, ghost_in[i]), 2)
     from_west = jnp.dot(s_in[0], w_in[0], preferred_element_type=F32)
     from_east = jnp.dot(s_in[lon + 1], w_in[2], preferred_element_type=F32)
-    extra = fold_part([zero_row] + ghost_in[1:lon + 1] + [zero_row], w_in)
-    sum_1 = jnp.zeros((lat, ch), F32)
-    sum_2 = jnp.zeros((lat, ch), F32)
-    for i in range(lon):
-        v = north(first[at(i)], extra[i:i + 1])
-        if i == 0:
-            v = v + from_west
-        if i == lon - 1:
-            v = v + from_east
+    fold[0] = fold_part([zero_row] + ghost_in[1:lon + 1] + [zero_row], w_in)
+    for i in range(lon + 2):
+        ghost_f[i] = ghost_in[i]
+    first[at(0)] += from_west
+    first[at(lon - 1)] += from_east
+
+    def first_lon(i, sums):
+        v = north(first[at(i)], fold[0, pl.ds(i, 1)])
         v = v.astype(BF16).astype(F32)
         first[at(i)] = v
         held = v * mask[at(i)]
-        sum_1 += held
-        sum_2 += held * v
-    stats1[me, 0:1] = jnp.sum(sum_1, axis=0, keepdims=True)
-    stats1[me, 1:2] = jnp.sum(sum_2, axis=0, keepdims=True)
-    send_stats(0, stats1)
-
-    for tap in range(9):
-        f, t = tap // 3, tap % 3
-        w = w_out[f, t * ch:(t + 1) * ch, :].astype(F32)
-        w_back[f, t * ch:(t + 1) * ch, :] = w.T.astype(BF16)
+        return sums[0] + held, sums[1] + held * v
+    zeros = jnp.zeros((lat, ch), F32)
+    sum_1, sum_2 = lax.fori_loop(0, lon, first_lon, (zeros, zeros))
+    stats[0, me, 0:1] = jnp.sum(sum_1, axis=0, keepdims=True)
+    stats[0, me, 1:2] = jnp.sum(sum_2, axis=0, keepdims=True)
+    send_stats(0)
+
+    def turn(f):
+        for t in range(3):
+            w = w_out[f, t * ch:(t + 1) * ch, :].astype(F32)
+            w_back[f, t * ch:(t + 1) * ch, :] = w.T.astype(BF16)
+    loop(0, 3, turn)
+
     count = zero_row
     for k in range(nz):
         packet = rows1[k].astype(F32)
@@ -259,73 +284,61 @@
 
     for c in cols_t:
         c.wait_recv()
-    for i in range(lon + 2):
-        if i == 0:
-            v = wests[1].astype(F32)
-        elif i == lon + 1:
-            v = easts[1].astype(F32)
-        else:
-            v = target[0, i - 1].astype(F32) * mask[at(i - 1)]
-        v = scaled(v)
+    def base_dout(i, v):
         put(s_dout, i, shift_up(v, zero_row), 0)
         put(s_dout, i, v, 1)
         put(s_dout, i, shift_down(v), 2)
-        if 0 < i <= lon and i % 2 == 0:
-            pair = jnp.concatenate([earlier, v], axis=0)
-            dout_t[:, (i - 2) * lat:i * lat] = pair.T.astype(BF16)
-        earlier = v
+
+    def lanes(k):
+        return pl.ds(pl.multiple_of(k * 2 * lat, 2 * lat), 2 * lat)
+
+    def dout_pair(k):
+        pair = [scaled(target[0, 2 * k + t].astype(F32)) for t in range(2)]
+        for t in range(2):
+            base_dout(2 * k + t + 1, pair[t])
+        dout_t[:, lanes(k)] = jnp.concatenate(pair, axis=0).T.astype(BF16)
+    loop(0, lon // 2, dout_pair)
+    base_dout(0, scaled(wests[1].astype(F32)))
+    base_dout(lon + 1, scaled(easts[1].astype(F32)))
     ghost_dout = [scaled(v) for v in ghosts(rows1, lon)]
-    total = conv(s_dout, w_back, (2, 1, 0))
-    extra = fold_part(ghost_dout, w_back)
-    for i in range(lon):
-        dact[at(i)] = north(total[i * lat:(i + 1) * lat], extra[i:i + 1])
-    for i in range(lon):
+    conv(s_dout, w_back, dact, (2, 1, 0))
+    fold[1] = fold_part(ghost_dout, w_back)
+
+    def finish_lon(i):
+        dact[at(i)] = north(dact[at(i)], fold[1, pl.ds(i, 1)]) * mask[at(i)]
         v = s_in[i + 1, :, ch:2 * ch].astype(F32)
-        put(s_in, i + 1, shift_up(v, ghost_in[i + 1]), 2)
-
-    recv_stats(0, stats1)
-
-    def gathered(buf):
-        acc = buf[0]
-        for k in range(1, nd):
-            acc = acc + buf[k]
-        return acc
-
-    acc = gathered(stats1)
+        put(s_in, i + 1, shift_up(v, ghost_f[i + 1]), 2)
+    loop(0, lon, finish_lon)
+
+    acc = recv_stats(0)
     mean = acc[0:1] / count
     var = acc[1:2] / count - mean * mean
     inverse = lax.rsqrt(var + 1e-05)
     gains = gain[...]
     offsets = offset[...]
 
-    sum_off = zero_row
-    sum_gain = zero_row
-    last = []
-    for i in range(lon):
+    def act_lon(i, sums):
         xhat = (first[at(i)] - mean) * inverse
         act, slope = gelu_parts(gains * xhat + offsets)
-        act = (act * mask[at(i)]).astype(BF16)
-        d = dact[at(i)] * mask[at(i)] * slope
+        d = dact[at(i)] * slope
         dpre[at(i)] = d
-        sum_off += jnp.sum(d, axis=0, keepdims=True)
-        sum_gain += jnp.sum(d * xhat, axis=0, keepdims=True)
-        s_act[i + 1, :, ch:2 * ch] = act
-        last.append(act.astype(F32)[lat - 1:])
-        if i == 0:
-            heads[2] = act
-        if i == lon - 1:
-            tails[2] = act
-    stats2[me, 0:1] = sum_off
-    stats2[me, 1:2] = sum_gain
-    send_stats(1, stats2)
+        s_act[i + 1, :, ch:2 * ch] = (act * mask[at(i)]).astype(BF16)
+        return sums[0] + d, sums[1] + d * xhat
+    sum_1, sum_2 = lax.fori_loop(0, lon, act_lon, (zeros, zeros))
+    sum_off = jnp.sum(sum_1, axis=0, keepdims=True)
+    sum_gain = jnp.sum(sum_2, axis=0, keepdims=True)
+    stats[1, me, 0:1] = sum_off
+    stats[1, me, 1:2] = sum_gain
+    send_stats(1)
+    heads[2] = s_act[1, :, ch:2 * ch]
+    tails[2] = s_act[lon, :, ch:2 * ch]
+    last = [s_act[i + 1, lat - 16:, ch:2 * ch].astype(F32)[15:] for i in range(lon)]
     rows2[z] = jnp.concatenate(last + [jnp.zeros((lon, ch), F32)], axis=0).astype(BF16)
     cols2 = col_copies(2)
     for c in cols2:
         c.start()
     send_rows(1, rows2)
 
-    for i in range(1, lon + 1):
-        put(s_act, i, shift_down(s_act[i, :, ch:2 * ch].astype(F32)), 0)
     for c in cols2:
         c.wait_recv()
     recv_rows(1, rows2)
@@ -333,27 +346,30 @@
     s_act[0, :, ch:2 * ch] = wests[2]
     s_act[lon + 1, :, ch:2 * ch] = easts[2]
     for i in range(lon + 2):
+        ghost_a[i] = ghost_act[i]
+
+    def act_shifts(i):
         v = s_act[i, :, ch:2 * ch].astype(F32)
-        if i == 0 or i == lon + 1:
-            put(s_act, i, shift_down(v), 0)
-        put(s_act, i, shift_up(v, ghost_act[i]), 2)
+        put(s_act, i, shift_down(v), 0)
+        put(s_act, i, shift_up(v, ghost_a[i]), 2)
+    loop(0, lon + 2, act_shifts)
 
     share = ch // nb
     live = 9 * share
     padded = units * 16 * nz
 
     def rows_of(f):
-        return pl.ds(3 * f * share, 3 * share)
+        return pl.ds(pl.multiple_of(3 * f * share, 16), 3 * share)
 
     def tap_grad(which, s, d_t, part, pair):
-        for f in range(3):
-            g = jnp.dot(d_t, window(s, f), preferred_element_type=F32).astype(BF16)
+        def one_f(f):
+            g = jnp.dot(d_t[...], window(s, f), preferred_element_type=F32).astype(BF16)
             for t in range(3):
-                tap = 3 * f + t
+                row = pl.ds(pl.multiple_of((3 * f + t) * share, 16), share)
                 for k in range(nb):
-                    part[k % 2, k // 2, tap * share:(tap + 1) * share, :] = (
-                        g[k * share:(k + 1) * share, t * ch:(t + 1) * ch])
+                    part[k % 2, k // 2, row, :] = g[k * share:(k + 1) * share, t * ch:(t + 1) * ch]
             pair_copy(which, f, part, pair).start()
+        loop(0, 3, one_f)
 
     def pair_copy(which, f, part, pair):
         return copy(part.at[other, :, rows_of(f)], pair.at[:, rows_of(f)],
@@ -373,7 +389,7 @@
                     full_sems.at[which, 1, slot], peer, b)
 
     def after_pair(which, part, pair, half, cross):
-        for f in range(3):
+        def one_f(f):
             pair_copy(which, f, part, pair).wait_recv()
             for x in range(nx):
                 half[x, rows_of(f)] = (
@@ -384,6 +400,7 @@
                 x = lax.rem(col + k, nx)
                 cross_copy(which, f, half, cross, col, x, x).start()
             over(nx, one)
+        loop(0, 3, one_f)
 
     def after_cross(which, half, cross, mine, ring):
         acc = half[col].astype(F32)
@@ -436,31 +453,36 @@
             full_copy(which, full, z, peer).wait_send()
         over(nz, one_z)
 
-    tap_grad(0, s_act, dout_t[...], part_a, pair_a)
-
-    recv_stats(1, stats2)
-    acc = gathered(stats2)
+    tap_grad(0, s_act, dout_t, part_a, pair_a)
+
+    acc = recv_stats(1)
     off_total = acc[0:1]
     gain_total = acc[1:2]
     offset_gradient[...] = off_total
     gain_gradient[...] = gain_total
     stores[3].start()
     stores[4].start()
-    for i in range(0, lon, 2):
+    scale_in = gains * inverse
+    off_mean = off_total / count
+    gain_mean = gain_total / count
+
+    def dfirst_pair(k):
         pieces = []
-        for j in (i, i + 1):
+        for j in (2 * k, 2 * k + 1):
             xhat = (first[at(j)] - mean) * inverse
-            pieces.append(mask[at(j)] * gains * inverse * (
-                dpre[at(j)] - (off_total + xhat * gain_total) / count))
-        pair = jnp.concatenate(pieces, axis=0)
-        dout_t[:, i * lat:(i + 2) * lat] = pair.T.astype(BF16)
+            pieces.append(mask[at(j)] * scale_in * (dpre[at(j)] - (off_mean + xhat * gain_mean)))
+        dout_t[:, lanes(k)] = jnp.concatenate(pieces, axis=0).T.astype(BF16)
+    loop(0, lon // 2, dfirst_pair)
     after_pair(0, part_a, pair_a, half_a, cross_a)
-    tap_grad(1, s_in, dout_t[...], part_b, pair_b)
+    tap_grad(1, s_in, dout_t, part_b, pair_b)
     after_cross(0, half_a, cross_a, mine_a, ring_a)
     after_pair(1, part_b, pair_b, half_b, cross_b)
 
-    total = conv(s_act, w_out)
-    output[0] = (total * mask[...]).astype(BF16).reshape(lon, lat, ch)
+    conv(s_act, w_out, dact)
+
+    def out_lon(i):
+        output[0, i] = (dact[at(i)] * mask[at(i)]).astype(BF16)
+    loop(0, lon, out_lon)
     stores[0].start()
 
     after_ring(0, mine_a, ring_a, full_a)
@@ -475,8 +497,8 @@
         c.wait_send()
     drain_rows(0, rows1)
     drain_rows(1, rows2)
-    drain_stats(0, stats1)
-    drain_stats(1, stats2)
+    drain_stats(0)
+    drain_stats(1)
     drain(0, part_a, pair_a, half_a, cross_a, mine_a, ring_a, full_a)
     drain(1, part_b, pair_b, half_b, cross_b, mine_b, ring_b, full_b)
     for store in stores:
@@ -484,11 +506,15 @@
 
 
 def writer(*refs):
-    sems = refs[-1]
-    copies = [pltpu.make_async_copy(refs[k], refs[5 + k], sems.at[k]) for k in range(5)]
-    for c in copies:
+    sources, results, held, sems = refs[:5], refs[5:10], refs[10:15], refs[15]
+    loads = [pltpu.make_async_copy(sources[k], held[k], sems.at[0, k]) for k in range(5)]
+    stores = [pltpu.make_async_copy(held[k], results[k], sems.at[1, k]) for k in range(5)]
+    for c in loads:
         c.start()
-    for c in copies:
+    for load, store in zip(loads, stores):
+        load.wait()
+        store.start()
+    for c in stores:
         c.wait()
 
 
@@ -536,8 +562,11 @@
         vm((nz, 16, ch), BF16),
         vm((3, lat, ch), BF16), vm((3, lat, ch), BF16),
         vm((3, lat, ch), BF16), vm((3, lat, ch), BF16),
-        vm((nd, 2, ch), F32),
-        vm((nd, 2, ch), F32),
+        vm((2, nd, 2, ch), F32),
+        vm((lon + 2, 1, ch), F32),
+        vm((lon + 2, 1, ch), F32),
+        vm((lon + 2, 1, ch), F32),
+        vm((2, 2 * lon, ch), F32),
         *reduction,
         *reduction,
         dma((7,)),
@@ -578,7 +607,7 @@
         out_shape=tuple(jax.ShapeDtypeStruct(r.shape, r.dtype) for r in results),
         in_specs=[anywhere] * 5,
         out_specs=(anywhere,) * 5,
-        scratch_shapes=[dma((5,))],
+        scratch_shapes=[vm(r.shape, r.dtype) for r in results] + [dma((2, 5))],
         compiler_params=pltpu.CompilerParams(vmem_limit_bytes=limit),
     )(*results)
 

time: 53.7 us -> 41.7 us (0.78)
  Pallas kernels: 52.8 us -> 40.8 us
    pallas_call x1, Pallas kernels: 14.1 us -> 1.8 us  [body(): pl.pallas_call(writer, out_shape=tuple((jax.ShapeDtypeStruct(r.shape, r.d...]
where the time goes in v4:
time: 41.7 us; the launch traced here: 41.5 us
  Pallas kernels  40.8 us (98%)
  between operations  0.64 us (2%)
    pallas_call x1, Pallas kernels, body(): pl.pallas_call(functools.partial(kernel, nz, nb, lon, lat, ch, units), ou...  39 us
    pallas_call x1, Pallas kernels, body(): pl.pallas_call(writer, out_shape=tuple((jax.ShapeDtypeStruct(r.shape, r.d...  1.8 us

profile of v4, /device:TPU:0, one launch (start us, length us, event | category | flops | bytes accessed | tf_op | source)
XLA Modules:
  0.0 41.5 jit_solution(7486216531777033377)
XLA Ops:
  0.6 39.0 %shard_map.110 = (bf16[1,8,64,128]{3,2,1,0:T(8,128)(2,1)}, f32[288,128]{1,0:T(8,128)}, f32[288,128]{1,0:T(8,128)}, f32[1,128]{1,0:T(1,128)}, f32[1,128]{1,0:T(1,128)}) custom-call(bf16[1,8,64,128]{3,2,1,0:T(8,128)(2,1)} %fields_h.1, s32[8,64]{1,0:T(8,128)} %land_h.1, bf16[3,384,128]{2,1,0:T(8,128)(2,1)} %bitcast.12, bf16[3,384,128]{2,1,0:T(8,128)(2,1)} %bitcast.13, ...), custom_call_target="tpu_custom_call" | custom-call | tf_op jit(solution)/shard_map/pallas_call | solution.py:584
  39.7 1.8 %shard_map.111 = (bf16[1,8,64,128]{3,2,1,0:T(8,128)(2,1)}, f32[288,128]{1,0:T(8,128)}, f32[288,128]{1,0:T(8,128)}, f32[1,128]{1,0:T(1,128)}, f32[1,128]{1,0:T(1,128)}) custom-call(bf16[1,8,64,128]{3,2,1,0:T(8,128)(2,1)} %get-tuple-element.15.refs_0_, f32[288,128]{1,0:T(8,128)} %get-tuple-element.16.refs_1_, f32[288,128]{1,0:T(8,128)} %get-tuple-element.17.refs_2_, ...), custom_call_target="tpu_custom_call" | custom-call | tf_op jit(solution)/shard_map/pallas_call | solution.py:605

commit v5 on v4

--- a/solution.py
+++ b/solution.py
@@ -30,19 +30,16 @@
     mask, first, dact, dpre, s_in, s_act, s_dout, w_back, dout_t,
     rows1, rows2, heads, tails, wests, easts,
     stats, ghost_f, ghost_d, ghost_a, fold,
-    part_a, pair_a, half_a, cross_a, mine_a, ring_a, full_a,
-    part_b, pair_b, half_b, cross_b, mine_b, ring_b, full_b,
-    load_sems, store_sems, row_sems, col_sems, stat_sems, pair_sems, cross_sems, ring_sems, full_sems,
+    acc_a, north_t,
+    part_a, peer_a, mine_a, ring_a, full_a,
+    part_b, peer_b, mine_b, ring_b, full_b,
+    load_sems, store_sems, row_sems, col_sems, stat_sems, part_sems, ring_sems, full_sems,
 ):
     nd = nz * nb
-    nx = nb // 2
     cells = lon * lat
     z = lax.axis_index("space")
     b = lax.axis_index("batch")
     me = z * nb + b
-    core = lax.rem(b, 2)
-    col = b // 2
-    other = 1 - core
 
     def device(zz, bb):
         return {"space": zz, "batch": bb}
@@ -162,7 +159,6 @@
         s[i, :, lane * ch:(lane + 1) * ch] = v.astype(BF16)
 
     loads[1].wait()
-    loads[2].wait()
     def base(s, i, v):
         put(s, i, shift_down(v), 0)
         put(s, i, v, 1)
@@ -170,8 +166,20 @@
 
     def mask_lon(i):
         base(s_in, i + 1, fields[0, i].astype(F32) * mask[at(i)])
+    loop(0, lon, mask_lon)
+    heads[0] = s_in[1, :, ch:2 * ch]
+    tails[0] = s_in[lon, :, ch:2 * ch]
+    cols1 = col_copies(0)
+    cols_t = col_copies(1)
+    pl.semaphore_wait(barrier, nd - 1)
+    for c in cols1:
+        c.start()
+
+    loads[2].wait()
+
+    def mask_target(i):
         target[0, i] = (target[0, i].astype(F32) * mask[at(i)]).astype(BF16)
-    loop(0, lon, mask_lon)
+    loop(0, lon, mask_target)
 
     halves = []
     for h in range(2):
@@ -181,16 +189,9 @@
         [s_in[i + 1, lat - 16:, ch:2 * ch].astype(F32)[15:] for i in range(lon)]
         + [target[0, i, lat - 16:].astype(F32)[15:] for i in range(lon)] + halves, axis=0
     ).astype(BF16)
-    heads[0] = s_in[1, :, ch:2 * ch]
-    tails[0] = s_in[lon, :, ch:2 * ch]
     heads[1] = target[0, 0]
     tails[1] = target[0, lon - 1]
 
-    cols1 = col_copies(0)
-    cols_t = col_copies(1)
-    pl.semaphore_wait(barrier, nd - 1)
-    for c in cols1:
-        c.start()
     send_rows(0, rows1)
     for c in cols_t:
         c.start()
@@ -301,6 +302,9 @@
     base_dout(0, scaled(wests[1].astype(F32)))
     base_dout(lon + 1, scaled(easts[1].astype(F32)))
     ghost_dout = [scaled(v) for v in ghosts(rows1, lon)]
+    north_d = [s_dout[i + 1, lat - 16:, ch:2 * ch].astype(F32)[15:] for i in range(lon)]
+    north_t[...] = jnp.concatenate(
+        north_d + [jnp.zeros((ch - lon, ch), F32)], axis=0).T.astype(BF16)
     conv(s_dout, w_back, dact, (2, 1, 0))
     fold[1] = fold_part(ghost_dout, w_back)
 
@@ -322,7 +326,7 @@
         act, slope = gelu_parts(gains * xhat + offsets)
         d = dact[at(i)] * slope
         dpre[at(i)] = d
-        s_act[i + 1, :, ch:2 * ch] = (act * mask[at(i)]).astype(BF16)
+        base(s_act, i + 1, (act * mask[at(i)]).astype(BF16).astype(F32))
         return sums[0] + d, sums[1] + d * xhat
     sum_1, sum_2 = lax.fori_loop(0, lon, act_lon, (zeros, zeros))
     sum_off = jnp.sum(sum_1, axis=0, keepdims=True)
@@ -339,20 +343,34 @@
         c.start()
     send_rows(1, rows2)
 
+    for i in (0, lon + 1):
+        s_act[i] = jnp.zeros((lat, 3 * ch), BF16)
+
+    def own_a(f):
+        acc_a[f] = jnp.dot(dout_t[...], window(s_act, f), preferred_element_type=F32)
+    loop(0, 3, own_a)
+
     for c in cols2:
         c.wait_recv()
     recv_rows(1, rows2)
     ghost_act = ghosts(rows2, 0)
-    s_act[0, :, ch:2 * ch] = wests[2]
-    s_act[lon + 1, :, ch:2 * ch] = easts[2]
     for i in range(lon + 2):
         ghost_a[i] = ghost_act[i]
-
-    def act_shifts(i):
-        v = s_act[i, :, ch:2 * ch].astype(F32)
+    for i, v in ((0, wests[2].astype(F32)), (lon + 1, easts[2].astype(F32))):
         put(s_act, i, shift_down(v), 0)
-        put(s_act, i, shift_up(v, ghost_a[i]), 2)
-    loop(0, lon + 2, act_shifts)
+        put(s_act, i, v, 1)
+        put(s_act, i, shift_up(v, ghost_act[i]), 2)
+    blank = jnp.zeros((lat, 3 * ch), BF16)
+    acc_a[0] += jnp.dot(dout_t[:, 0:2 * lat], jnp.concatenate([s_act[0], blank], axis=0),
+                        preferred_element_type=F32)
+    acc_a[2] += jnp.dot(dout_t[:, cells - 2 * lat:],
+                        jnp.concatenate([blank, s_act[lon + 1]], axis=0),
+                        preferred_element_type=F32)
+    inner = [zero_row] + ghost_act[1:lon + 1] + [zero_row]
+    for f in range(3):
+        piece = jnp.concatenate(inner[f:f + lon] + [jnp.zeros((ch - lon, ch), F32)], axis=0)
+        acc_a[f, :, 2 * ch:] += jnp.dot(north_t[...], piece.astype(BF16),
+                                        preferred_element_type=F32)
 
     share = ch // nb
     live = 9 * share
@@ -361,24 +379,20 @@
     def rows_of(f):
         return pl.ds(pl.multiple_of(3 * f * share, 16), 3 * share)
 
-    def tap_grad(which, s, d_t, part, pair):
-        def one_f(f):
-            g = jnp.dot(d_t[...], window(s, f), preferred_element_type=F32).astype(BF16)
-            for t in range(3):
-                row = pl.ds(pl.multiple_of((3 * f + t) * share, 16), share)
-                for k in range(nb):
-                    part[k % 2, k // 2, row, :] = g[k * share:(k + 1) * share, t * ch:(t + 1) * ch]
-            pair_copy(which, f, part, pair).start()
-        loop(0, 3, one_f)
-
-    def pair_copy(which, f, part, pair):
-        return copy(part.at[other, :, rows_of(f)], pair.at[:, rows_of(f)],
-                    pair_sems.at[which, 0, f], pair_sems.at[which, 1, f], z, 2 * col + other)
-
-    def cross_copy(which, f, half, cross, slot, peer, x):
-        return copy(half.at[peer, rows_of(f)], cross.at[slot, rows_of(f)],
-                    cross_sems.at[which, 0, f, peer], cross_sems.at[which, 1, f, slot],
-                    z, 2 * x + core)
+    def part_copy(which, f, part, peers, slot, peer):
+        return copy(part.at[peer, rows_of(f)], peers.at[slot, rows_of(f)],
+                    part_sems.at[which, 0, f, peer], part_sems.at[which, 1, f, slot], z, peer)
+
+    def send_part(which, f, g, part, peers):
+        for t in range(3):
+            row = pl.ds(pl.multiple_of((3 * f + t) * share, 16), share)
+            for k in range(nb):
+                part[k, row, :] = g[k * share:(k + 1) * share, t * ch:(t + 1) * ch].astype(BF16)
+
+        def one(k):
+            peer = lax.rem(b + k, nb)
+            part_copy(which, f, part, peers, b, peer).start()
+        over(nb, one)
 
     def ring_copy(which, mine, ring, slot, peer):
         return copy(mine.at[peer], ring.at[slot], ring_sems.at[which, 0, peer],
@@ -388,27 +402,13 @@
         return copy(full.at[slot], full.at[slot], full_sems.at[which, 0, peer],
                     full_sems.at[which, 1, slot], peer, b)
 
-    def after_pair(which, part, pair, half, cross):
-        def one_f(f):
-            pair_copy(which, f, part, pair).wait_recv()
-            for x in range(nx):
-                half[x, rows_of(f)] = (
-                    part[core, x, rows_of(f)].astype(F32) + pair[x, rows_of(f)].astype(F32)
-                ).astype(BF16)
-
-            def one(k):
-                x = lax.rem(col + k, nx)
-                cross_copy(which, f, half, cross, col, x, x).start()
-            over(nx, one)
-        loop(0, 3, one_f)
-
-    def after_cross(which, half, cross, mine, ring):
-        acc = half[col].astype(F32)
-        for k in range(1, nx):
-            x = lax.rem(col + k, nx)
+    def after_part(which, part, peers, mine, ring):
+        acc = part[b].astype(F32)
+        for k in range(1, nb):
+            src = lax.rem(b + k, nb)
             for f in range(3):
-                cross_copy(which, f, half, cross, x, x, x).wait_recv()
-            acc = acc + cross[x].astype(F32)
+                part_copy(which, f, part, peers, src, src).wait_recv()
+            acc = acc + peers[src].astype(F32)
         if padded > live:
             acc = jnp.concatenate([acc, jnp.zeros((padded - live, ch), F32)], axis=0)
         for k in range(nz):
@@ -438,14 +438,12 @@
         over(nz, one)
         out[...] = full[...].reshape(padded, ch)[0:live].astype(F32)
 
-    def drain(which, part, pair, half, cross, mine, ring, full):
+    def drain(which, part, peers, mine, ring, full):
         for f in range(3):
-            pair_copy(which, f, part, pair).wait_send()
-
-            def one_x(k):
-                x = lax.rem(col + k, nx)
-                cross_copy(which, f, half, cross, col, x, x).wait_send()
-            over(nx, one_x)
+            def one_b(k):
+                peer = lax.rem(b + k, nb)
+                part_copy(which, f, part, peers, b, peer).wait_send()
+            over(nb, one_b)
 
         def one_z(k):
             peer = lax.rem(z + k, nz)
@@ -453,7 +451,7 @@
             full_copy(which, full, z, peer).wait_send()
         over(nz, one_z)
 
-    tap_grad(0, s_act, dout_t, part_a, pair_a)
+    loop(0, 3, lambda f: send_part(0, f, acc_a[f], part_a, peer_a))
 
     acc = recv_stats(1)
     off_total = acc[0:1]
@@ -473,11 +471,17 @@
             pieces.append(mask[at(j)] * scale_in * (dpre[at(j)] - (off_mean + xhat * gain_mean)))
         dout_t[:, lanes(k)] = jnp.concatenate(pieces, axis=0).T.astype(BF16)
     loop(0, lon // 2, dfirst_pair)
-    after_pair(0, part_a, pair_a, half_a, cross_a)
-    tap_grad(1, s_in, dout_t, part_b, pair_b)
-    after_cross(0, half_a, cross_a, mine_a, ring_a)
-    after_pair(1, part_b, pair_b, half_b, cross_b)
-
+
+    def tap_b(f):
+        g = jnp.dot(dout_t[...], window(s_in, f), preferred_element_type=F32)
+        send_part(1, f, g, part_b, peer_b)
+    loop(0, 3, tap_b)
+    after_part(0, part_a, peer_a, mine_a, ring_a)
+
+    def finish_act(i):
+        v = s_act[i + 1, :, ch:2 * ch].astype(F32)
+        put(s_act, i + 1, shift_up(v, ghost_a[i + 1]), 2)
+    loop(0, lon, finish_act)
     conv(s_act, w_out, dact)
 
     def out_lon(i):
@@ -486,7 +490,7 @@
     stores[0].start()
 
     after_ring(0, mine_a, ring_a, full_a)
-    after_cross(1, half_b, cross_b, mine_b, ring_b)
+    after_part(1, part_b, peer_b, mine_b, ring_b)
     after_ring(1, mine_b, ring_b, full_b)
     after_full(0, full_a, grad_out)
     stores[2].start()
@@ -499,8 +503,8 @@
     drain_rows(1, rows2)
     drain_stats(0)
     drain_stats(1)
-    drain(0, part_a, pair_a, half_a, cross_a, mine_a, ring_a, full_a)
-    drain(1, part_b, pair_b, half_b, cross_b, mine_b, ring_b, full_b)
+    drain(0, part_a, peer_a, mine_a, ring_a, full_a)
+    drain(1, part_b, peer_b, mine_b, ring_b, full_b)
     for store in stores:
         store.wait()
 
@@ -521,16 +525,13 @@
 def body(nz, nb, fields, land, conv_in, conv_out, gain, offset, target):
     lon, lat, ch = fields.shape[1:]
     nd = nz * nb
-    nx = nb // 2
     share = ch // nb
     units = -(-(9 * share // 16) // nz)
     padded = units * 16 * nz
     vm = pltpu.VMEM
     reduction = [
-        vm((2, nx, 9 * share, ch), BF16),
-        vm((nx, 9 * share, ch), BF16),
-        vm((nx, 9 * share, ch), BF16),
-        vm((nx, 9 * share, ch), BF16),
+        vm((nb, 9 * share, ch), BF16),
+        vm((nb, 9 * share, ch), BF16),
         vm((nz, units * 16, ch), BF16),
         vm((nz, units * 16, ch), BF16),
         vm((nz, units * 16, ch), BF16),
@@ -567,6 +568,8 @@
         vm((lon + 2, 1, ch), F32),
         vm((lon + 2, 1, ch), F32),
         vm((2, 2 * lon, ch), F32),
+        vm((3, ch, 3 * ch), F32),
+        vm((ch, ch), BF16),
         *reduction,
         *reduction,
         dma((7,)),
@@ -574,8 +577,7 @@
         dma((2, 2, nz)),
         dma((3, 2, 2)),
         dma((2, 2, nd)),
-        dma((2, 2, 3)),
-        dma((2, 2, 3, nx)),
+        dma((2, 2, 3, nb)),
         dma((2, 2, nz)),
         dma((2, 2, nz)),
     ]

time: 41.7 us -> 43.4 us (1.041)
  Pallas kernels: 40.8 us -> 42.5 us
    pallas_call x1, Pallas kernels: 39 us -> 40.7 us  [body(): pl.pallas_call(functools.partial(kernel, nz, nb, lon, lat, ch, units), ou...]
where the time goes in v5:
time: 43.4 us; the launch traced here: 43.2 us
  Pallas kernels  42.5 us (98%)
  between operations  0.64 us (1%)
    pallas_call x1, Pallas kernels, body(): pl.pallas_call(functools.partial(kernel, nz, nb, lon, lat, ch, units), ou...  40.7 us
    pallas_call x1, Pallas kernels, body(): pl.pallas_call(writer, out_shape=tuple((jax.ShapeDtypeStruct(r.shape, r.d...  1.8 us

profile of v5, /device:TPU:0, one launch (start us, length us, event | category | flops | bytes accessed | tf_op | source)
XLA Modules:
  0.0 43.2 jit_solution(14497330397976622031)
XLA Ops:
  0.6 40.7 %shard_map.110 = (bf16[1,8,64,128]{3,2,1,0:T(8,128)(2,1)}, f32[288,128]{1,0:T(8,128)}, f32[288,128]{1,0:T(8,128)}, f32[1,128]{1,0:T(1,128)}, f32[1,128]{1,0:T(1,128)}) custom-call(bf16[1,8,64,128]{3,2,1,0:T(8,128)(2,1)} %fields_h.1, s32[8,64]{1,0:T(8,128)} %land_h.1, bf16[3,384,128]{2,1,0:T(8,128)(2,1)} %bitcast.12, bf16[3,384,128]{2,1,0:T(8,128)(2,1)} %bitcast.13, ...), custom_call_target="tpu_custom_call" | custom-call | tf_op jit(solution)/shard_map/pallas_call | solution.py:586
  41.4 1.8 %shard_map.111 = (bf16[1,8,64,128]{3,2,1,0:T(8,128)(2,1)}, f32[288,128]{1,0:T(8,128)}, f32[288,128]{1,0:T(8,128)}, f32[1,128]{1,0:T(1,128)}, f32[1,128]{1,0:T(1,128)}) custom-call(bf16[1,8,64,128]{3,2,1,0:T(8,128)(2,1)} %get-tuple-element.15.refs_0_, f32[288,128]{1,0:T(8,128)} %get-tuple-element.16.refs_1_, f32[288,128]{1,0:T(8,128)} %get-tuple-element.17.refs_2_, ...), custom_call_target="tpu_custom_call" | custom-call | tf_op jit(solution)/shard_map/pallas_call | solution.py:607

commit v6 on v5

--- a/solution.py
+++ b/solution.py
@@ -31,15 +31,19 @@
     rows1, rows2, heads, tails, wests, easts,
     stats, ghost_f, ghost_d, ghost_a, fold,
     acc_a, north_t,
-    part_a, peer_a, mine_a, ring_a, full_a,
-    part_b, peer_b, mine_b, ring_b, full_b,
-    load_sems, store_sems, row_sems, col_sems, stat_sems, part_sems, ring_sems, full_sems,
+    part_a, pair_a, half_a, cross_a, mine_a, ring_a, full_a,
+    part_b, pair_b, half_b, cross_b, mine_b, ring_b, full_b,
+    load_sems, store_sems, row_sems, col_sems, stat_sems, pair_sems, cross_sems, ring_sems, full_sems,
 ):
     nd = nz * nb
+    nx = nb // 2
     cells = lon * lat
     z = lax.axis_index("space")
     b = lax.axis_index("batch")
     me = z * nb + b
+    core = lax.rem(b, 2)
+    col = b // 2
+    other = 1 - core
 
     def device(zz, bb):
         return {"space": zz, "batch": bb}
@@ -202,16 +206,16 @@
     def window(s, f):
         return s[pl.ds(f, lon)].reshape(cells, 3 * ch)
 
+    def conv_half(s, w, out, h, order=(0, 1, 2)):
+        part_lon = lon // 2
+        acc = jnp.zeros((part_lon * lat, ch), F32)
+        for f in range(3):
+            piece = s[pl.ds(h * part_lon + order[f], part_lon)].reshape(part_lon * lat, 3 * ch)
+            acc += jnp.dot(piece, w[f], preferred_element_type=F32)
+        out[pl.ds(pl.multiple_of(h * part_lon * lat, part_lon * lat), part_lon * lat)] = acc
+
     def conv(s, w, out, order=(0, 1, 2)):
-        part_lon = lon // 2
-
-        def half(h):
-            acc = jnp.zeros((part_lon * lat, ch), F32)
-            for f in range(3):
-                piece = s[pl.ds(h * part_lon + order[f], part_lon)].reshape(part_lon * lat, 3 * ch)
-                acc += jnp.dot(piece, w[f], preferred_element_type=F32)
-            out[pl.ds(pl.multiple_of(h * part_lon * lat, part_lon * lat), part_lon * lat)] = acc
-        loop(0, 2, half)
+        loop(0, 2, lambda h: conv_half(s, w, out, h, order))
 
     def fold_part(rows, w):
         acc = jnp.zeros((2 * lon, ch), F32)
@@ -379,20 +383,22 @@
     def rows_of(f):
         return pl.ds(pl.multiple_of(3 * f * share, 16), 3 * share)
 
-    def part_copy(which, f, part, peers, slot, peer):
-        return copy(part.at[peer, rows_of(f)], peers.at[slot, rows_of(f)],
-                    part_sems.at[which, 0, f, peer], part_sems.at[which, 1, f, slot], z, peer)
-
-    def send_part(which, f, g, part, peers):
+    def pair_copy(which, f, part, pair):
+        return copy(part.at[other, :, rows_of(f)], pair.at[:, rows_of(f)],
+                    pair_sems.at[which, 0, f], pair_sems.at[which, 1, f], z, 2 * col + other)
+
+    def cross_copy(which, f, half, cross, slot, peer, x):
+        return copy(half.at[peer, rows_of(f)], cross.at[slot, rows_of(f)],
+                    cross_sems.at[which, 0, f, peer], cross_sems.at[which, 1, f, slot],
+                    z, 2 * x + core)
+
+    def send_part(which, f, g, part, pair):
         for t in range(3):
             row = pl.ds(pl.multiple_of((3 * f + t) * share, 16), share)
             for k in range(nb):
-                part[k, row, :] = g[k * share:(k + 1) * share, t * ch:(t + 1) * ch].astype(BF16)
-
-        def one(k):
-            peer = lax.rem(b + k, nb)
-            part_copy(which, f, part, peers, b, peer).start()
-        over(nb, one)
+                part[k % 2, k // 2, row, :] = (
+                    g[k * share:(k + 1) * share, t * ch:(t + 1) * ch].astype(BF16))
+        pair_copy(which, f, part, pair).start()
 
     def ring_copy(which, mine, ring, slot, peer):
         return copy(mine.at[peer], ring.at[slot], ring_sems.at[which, 0, peer],
@@ -402,13 +408,29 @@
         return copy(full.at[slot], full.at[slot], full_sems.at[which, 0, peer],
                     full_sems.at[which, 1, slot], peer, b)
 
-    def after_part(which, part, peers, mine, ring):
-        acc = part[b].astype(F32)
-        for k in range(1, nb):
-            src = lax.rem(b + k, nb)
+    def after_pair(which, part, pair, half, cross):
+        def one_f(f):
+            pair_copy(which, f, part, pair).wait_recv()
+
+            def summed(x):
+                return (part[core, x, rows_of(f)].astype(F32)
+                        + pair[x, rows_of(f)].astype(F32)).astype(BF16)
+
+            def one(k):
+                x = lax.rem(col + k, nx)
+                half[x, rows_of(f)] = summed(x)
+                cross_copy(which, f, half, cross, col, x, x).start()
+            over(nx, one)
+            half[col, rows_of(f)] = summed(col)
+        loop(0, 3, one_f)
+
+    def after_cross(which, half, cross, mine, ring):
+        acc = half[col].astype(F32)
+        for k in range(1, nx):
+            x = lax.rem(col + k, nx)
             for f in range(3):
-                part_copy(which, f, part, peers, src, src).wait_recv()
-            acc = acc + peers[src].astype(F32)
+                cross_copy(which, f, half, cross, x, x, x).wait_recv()
+            acc = acc + cross[x].astype(F32)
         if padded > live:
             acc = jnp.concatenate([acc, jnp.zeros((padded - live, ch), F32)], axis=0)
         for k in range(nz):
@@ -438,12 +460,14 @@
         over(nz, one)
         out[...] = full[...].reshape(padded, ch)[0:live].astype(F32)
 
-    def drain(which, part, peers, mine, ring, full):
+    def drain(which, part, pair, half, cross, mine, ring, full):
         for f in range(3):
-            def one_b(k):
-                peer = lax.rem(b + k, nb)
-                part_copy(which, f, part, peers, b, peer).wait_send()
-            over(nb, one_b)
+            pair_copy(which, f, part, pair).wait_send()
+
+            def one_x(k):
+                x = lax.rem(col + k, nx)
+                cross_copy(which, f, half, cross, col, x, x).wait_send()
+            over(nx, one_x)
 
         def one_z(k):
             peer = lax.rem(z + k, nz)
@@ -451,7 +475,7 @@
             full_copy(which, full, z, peer).wait_send()
         over(nz, one_z)
 
-    loop(0, 3, lambda f: send_part(0, f, acc_a[f], part_a, peer_a))
+    loop(0, 3, lambda f: send_part(0, f, acc_a[f], part_a, pair_a))
 
     acc = recv_stats(1)
     off_total = acc[0:1]
@@ -471,26 +495,28 @@
             pieces.append(mask[at(j)] * scale_in * (dpre[at(j)] - (off_mean + xhat * gain_mean)))
         dout_t[:, lanes(k)] = jnp.concatenate(pieces, axis=0).T.astype(BF16)
     loop(0, lon // 2, dfirst_pair)
+    after_pair(0, part_a, pair_a, half_a, cross_a)
 
     def tap_b(f):
         g = jnp.dot(dout_t[...], window(s_in, f), preferred_element_type=F32)
-        send_part(1, f, g, part_b, peer_b)
+        send_part(1, f, g, part_b, pair_b)
     loop(0, 3, tap_b)
-    after_part(0, part_a, peer_a, mine_a, ring_a)
 
     def finish_act(i):
         v = s_act[i + 1, :, ch:2 * ch].astype(F32)
         put(s_act, i + 1, shift_up(v, ghost_a[i + 1]), 2)
     loop(0, lon, finish_act)
-    conv(s_act, w_out, dact)
+    after_pair(1, part_b, pair_b, half_b, cross_b)
+    conv_half(s_act, w_out, dact, 0)
+    after_cross(0, half_a, cross_a, mine_a, ring_a)
+    conv_half(s_act, w_out, dact, 1)
+    after_cross(1, half_b, cross_b, mine_b, ring_b)
 
     def out_lon(i):
         output[0, i] = (dact[at(i)] * mask[at(i)]).astype(BF16)
     loop(0, lon, out_lon)
     stores[0].start()
-
     after_ring(0, mine_a, ring_a, full_a)
-    after_part(1, part_b, peer_b, mine_b, ring_b)
     after_ring(1, mine_b, ring_b, full_b)
     after_full(0, full_a, grad_out)
     stores[2].start()
@@ -503,8 +529,8 @@
     drain_rows(1, rows2)
     drain_stats(0)
     drain_stats(1)
-    drain(0, part_a, peer_a, mine_a, ring_a, full_a)
-    drain(1, part_b, peer_b, mine_b, ring_b, full_b)
+    drain(0, part_a, pair_a, half_a, cross_a, mine_a, ring_a, full_a)
+    drain(1, part_b, pair_b, half_b, cross_b, mine_b, ring_b, full_b)
     for store in stores:
         store.wait()
 
@@ -525,13 +551,16 @@
 def body(nz, nb, fields, land, conv_in, conv_out, gain, offset, target):
     lon, lat, ch = fields.shape[1:]
     nd = nz * nb
+    nx = nb // 2
     share = ch // nb
     units = -(-(9 * share // 16) // nz)
     padded = units * 16 * nz
     vm = pltpu.VMEM
     reduction = [
-        vm((nb, 9 * share, ch), BF16),
-        vm((nb, 9 * share, ch), BF16),
+        vm((2, nx, 9 * share, ch), BF16),
+        vm((nx, 9 * share, ch), BF16),
+        vm((nx, 9 * share, ch), BF16),
+        vm((nx, 9 * share, ch), BF16),
         vm((nz, units * 16, ch), BF16),
         vm((nz, units * 16, ch), BF16),
         vm((nz, units * 16, ch), BF16),
@@ -577,7 +606,8 @@
         dma((2, 2, nz)),
         dma((3, 2, 2)),
         dma((2, 2, nd)),
-        dma((2, 2, 3, nb)),
+        dma((2, 2, 3)),
+        dma((2, 2, 3, nx)),
         dma((2, 2, nz)),
         dma((2, 2, nz)),
     ]

time: 43.4 us -> 38.4 us (0.88)
  Pallas kernels: 42.5 us -> 37.6 us
    pallas_call x1, Pallas kernels: 40.7 us -> 35.8 us  [body(): pl.pallas_call(functools.partial(kernel, nz, nb, lon, lat, ch, units), ou...]
where the time goes in v6:
time: 38.4 us; the launch traced here: 38.2 us
  Pallas kernels  37.6 us (98%)
  between operations  0.64 us (2%)
    pallas_call x1, Pallas kernels, body(): pl.pallas_call(functools.partial(kernel, nz, nb, lon, lat, ch, units), ou...  35.8 us
    pallas_call x1, Pallas kernels, body(): pl.pallas_call(writer, out_shape=tuple((jax.ShapeDtypeStruct(r.shape, r.d...  1.8 us

profile of v6, /device:TPU:0, one launch (start us, length us, event | category | flops | bytes accessed | tf_op | source)
XLA Modules:
  0.0 38.2 jit_solution(13215145840318393025)
XLA Ops:
  0.6 35.8 %shard_map.110 = (bf16[1,8,64,128]{3,2,1,0:T(8,128)(2,1)}, f32[288,128]{1,0:T(8,128)}, f32[288,128]{1,0:T(8,128)}, f32[1,128]{1,0:T(1,128)}, f32[1,128]{1,0:T(1,128)}) custom-call(bf16[1,8,64,128]{3,2,1,0:T(8,128)(2,1)} %fields_h.1, s32[8,64]{1,0:T(8,128)} %land_h.1, bf16[3,384,128]{2,1,0:T(8,128)(2,1)} %bitcast.12, bf16[3,384,128]{2,1,0:T(8,128)(2,1)} %bitcast.13, ...), custom_call_target="tpu_custom_call" | custom-call | tf_op jit(solution)/shard_map/pallas_call | solution.py:616
  36.4 1.8 %shard_map.111 = (bf16[1,8,64,128]{3,2,1,0:T(8,128)(2,1)}, f32[288,128]{1,0:T(8,128)}, f32[288,128]{1,0:T(8,128)}, f32[1,128]{1,0:T(1,128)}, f32[1,128]{1,0:T(1,128)}) custom-call(bf16[1,8,64,128]{3,2,1,0:T(8,128)(2,1)} %get-tuple-element.15.refs_0_, f32[288,128]{1,0:T(8,128)} %get-tuple-element.16.refs_1_, f32[288,128]{1,0:T(8,128)} %get-tuple-element.17.refs_2_, ...), custom_call_target="tpu_custom_call" | custom-call | tf_op jit(solution)/shard_map/pallas_call | solution.py:637

commit v7 on v6

--- a/solution.py
+++ b/solution.py
@@ -22,7 +22,7 @@
 
 
 def kernel(
-    nz, nb, lon, lat, ch, units,
+    nz, nb, lon, lat, ch, depth,
     fields_h, land_h, w_in_h, w_out_h, gain_h, offset_h, target_h,
     output_h, grad_in_h, grad_out_h, gain_gradient_h, offset_gradient_h,
     output, grad_in, grad_out, gain_gradient, offset_gradient,
@@ -31,9 +31,9 @@
     rows1, rows2, heads, tails, wests, easts,
     stats, ghost_f, ghost_d, ghost_a, fold,
     acc_a, north_t,
-    part_a, pair_a, half_a, cross_a, mine_a, ring_a, full_a,
-    part_b, pair_b, half_b, cross_b, mine_b, ring_b, full_b,
-    load_sems, store_sems, row_sems, col_sems, stat_sems, pair_sems, cross_sems, ring_sems, full_sems,
+    part_a, pair_a, half_a, cross_a, mine_a, next_a, ring_a, full_a,
+    part_b, pair_b, half_b, cross_b, mine_b, next_b, ring_b, full_b,
+    load_sems, store_sems, row_sems, col_sems, stat_sems, pair_sems, cross_sems, next_sems, ring_sems, full_sems,
 ):
     nd = nz * nb
     nx = nb // 2
@@ -44,6 +44,10 @@
     core = lax.rem(b, 2)
     col = b // 2
     other = 1 - core
+    nh = nz // 2
+    side = lax.rem(z, 2)
+    duo = z // 2
+    facing_z = 2 * duo + 1 - side
 
     def device(zz, bb):
         return {"space": zz, "batch": bb}
@@ -378,7 +382,7 @@
 
     share = ch // nb
     live = 9 * share
-    padded = units * 16 * nz
+    padded = 2 * depth
 
     def rows_of(f):
         return pl.ds(pl.multiple_of(3 * f * share, 16), 3 * share)
@@ -400,13 +404,17 @@
                     g[k * share:(k + 1) * share, t * ch:(t + 1) * ch].astype(BF16))
         pair_copy(which, f, part, pair).start()
 
-    def ring_copy(which, mine, ring, slot, peer):
-        return copy(mine.at[peer], ring.at[slot], ring_sems.at[which, 0, peer],
-                    ring_sems.at[which, 1, slot], peer, b)
-
-    def full_copy(which, full, slot, peer):
-        return copy(full.at[slot], full.at[slot], full_sems.at[which, 0, peer],
-                    full_sems.at[which, 1, slot], peer, b)
+    def next_copy(which, mine, near):
+        return copy(mine.at[1 - side], near, next_sems.at[which, 0], next_sems.at[which, 1],
+                    facing_z, b)
+
+    def ring_copy(which, ring, slot, peer):
+        return copy(ring.at[slot], ring.at[slot], ring_sems.at[which, 0, peer],
+                    ring_sems.at[which, 1, slot], 2 * peer + side, b)
+
+    def full_copy(which, full, half):
+        return copy(full.at[half], full.at[half], full_sems.at[which, 0], full_sems.at[which, 1],
+                    facing_z, b)
 
     def after_pair(which, part, pair, half, cross):
         def one_f(f):
@@ -424,7 +432,7 @@
             half[col, rows_of(f)] = summed(col)
         loop(0, 3, one_f)
 
-    def after_cross(which, half, cross, mine, ring):
+    def after_cross(which, half, cross, mine, near):
         acc = half[col].astype(F32)
         for k in range(1, nx):
             x = lax.rem(col + k, nx)
@@ -433,34 +441,31 @@
             acc = acc + cross[x].astype(F32)
         if padded > live:
             acc = jnp.concatenate([acc, jnp.zeros((padded - live, ch), F32)], axis=0)
-        for k in range(nz):
-            mine[k] = acc[k * units * 16:(k + 1) * units * 16].astype(BF16)
-
+        for k in range(2):
+            mine[k] = acc[k * depth:(k + 1) * depth].astype(BF16)
+        next_copy(which, mine, near).start()
+
+    def after_next(which, mine, near, ring):
+        next_copy(which, mine, near).wait_recv()
+        ring[duo] = (mine[side].astype(F32) + near[...].astype(F32)).astype(BF16)
+        over(nh, lambda k: ring_copy(which, ring, duo, lax.rem(duo + k, nh)).start())
+
+    def after_ring(which, ring, full):
         def one(k):
-            peer = lax.rem(z + k, nz)
-            ring_copy(which, mine, ring, z, peer).start()
-        over(nz, one)
-
-    def after_ring(which, mine, ring, full):
-        acc = mine[z].astype(F32)
-        for k in range(1, nz):
-            src = lax.rem(z + k, nz)
-            ring_copy(which, mine, ring, src, src).wait_recv()
-            acc = acc + ring[src].astype(F32)
-        full[z] = acc.astype(BF16)
-
-        def one(k):
-            full_copy(which, full, z, lax.rem(z + k, nz)).start()
-        over(nz, one)
+            src = lax.rem(duo + k, nh)
+            ring_copy(which, ring, src, src).wait_recv()
+        over(nh, one)
+        acc = ring[0].astype(F32)
+        for k in range(1, nh):
+            acc = acc + ring[k].astype(F32)
+        full[side] = acc.astype(BF16)
+        full_copy(which, full, side).start()
 
     def after_full(which, full, out):
-        def one(k):
-            src = lax.rem(z + k, nz)
-            full_copy(which, full, src, src).wait_recv()
-        over(nz, one)
+        full_copy(which, full, 1 - side).wait_recv()
         out[...] = full[...].reshape(padded, ch)[0:live].astype(F32)
 
-    def drain(which, part, pair, half, cross, mine, ring, full):
+    def drain(which, part, pair, half, cross, mine, near, ring, full):
         for f in range(3):
             pair_copy(which, f, part, pair).wait_send()
 
@@ -469,11 +474,9 @@
                 cross_copy(which, f, half, cross, col, x, x).wait_send()
             over(nx, one_x)
 
-        def one_z(k):
-            peer = lax.rem(z + k, nz)
-            ring_copy(which, mine, ring, z, peer).wait_send()
-            full_copy(which, full, z, peer).wait_send()
-        over(nz, one_z)
+        next_copy(which, mine, near).wait_send()
+        over(nh, lambda k: ring_copy(which, ring, duo, lax.rem(duo + k, nh)).wait_send())
+        full_copy(which, full, side).wait_send()
 
     loop(0, 3, lambda f: send_part(0, f, acc_a[f], part_a, pair_a))
 
@@ -508,16 +511,18 @@
     loop(0, lon, finish_act)
     after_pair(1, part_b, pair_b, half_b, cross_b)
     conv_half(s_act, w_out, dact, 0)
-    after_cross(0, half_a, cross_a, mine_a, ring_a)
+    after_cross(0, half_a, cross_a, mine_a, next_a)
     conv_half(s_act, w_out, dact, 1)
-    after_cross(1, half_b, cross_b, mine_b, ring_b)
+    after_cross(1, half_b, cross_b, mine_b, next_b)
 
     def out_lon(i):
         output[0, i] = (dact[at(i)] * mask[at(i)]).astype(BF16)
     loop(0, lon, out_lon)
     stores[0].start()
-    after_ring(0, mine_a, ring_a, full_a)
-    after_ring(1, mine_b, ring_b, full_b)
+    after_next(0, mine_a, next_a, ring_a)
+    after_next(1, mine_b, next_b, ring_b)
+    after_ring(0, ring_a, full_a)
+    after_ring(1, ring_b, full_b)
     after_full(0, full_a, grad_out)
     stores[2].start()
     after_full(1, full_b, grad_in)
@@ -529,8 +534,8 @@
     drain_rows(1, rows2)
     drain_stats(0)
     drain_stats(1)
-    drain(0, part_a, pair_a, half_a, cross_a, mine_a, ring_a, full_a)
-    drain(1, part_b, pair_b, half_b, cross_b, mine_b, ring_b, full_b)
+    drain(0, part_a, pair_a, half_a, cross_a, mine_a, next_a, ring_a, full_a)
+    drain(1, part_b, pair_b, half_b, cross_b, mine_b, next_b, ring_b, full_b)
     for store in stores:
         store.wait()
 
@@ -553,17 +558,17 @@
     nd = nz * nb
     nx = nb // 2
     share = ch // nb
-    units = -(-(9 * share // 16) // nz)
-    padded = units * 16 * nz
+    depth = -(-9 * share // 32) * 16
     vm = pltpu.VMEM
     reduction = [
         vm((2, nx, 9 * share, ch), BF16),
         vm((nx, 9 * share, ch), BF16),
         vm((nx, 9 * share, ch), BF16),
         vm((nx, 9 * share, ch), BF16),
-        vm((nz, units * 16, ch), BF16),
-        vm((nz, units * 16, ch), BF16),
-        vm((nz, units * 16, ch), BF16),
+        vm((2, depth, ch), BF16),
+        vm((depth, ch), BF16),
+        vm((nz // 2, depth, ch), BF16),
+        vm((2, depth, ch), BF16),
     ]
     dma = pltpu.SemaphoreType.DMA
     scratch = [
@@ -608,13 +613,14 @@
         dma((2, 2, nd)),
         dma((2, 2, 3)),
         dma((2, 2, 3, nx)),
-        dma((2, 2, nz)),
-        dma((2, 2, nz)),
+        dma((2, 2)),
+        dma((2, 2, nz // 2)),
+        dma((2, 2)),
     ]
     anywhere = pl.BlockSpec(memory_space=pl.ANY)
     limit = 62 * 1024 * 1024
     results = pl.pallas_call(
-        functools.partial(kernel, nz, nb, lon, lat, ch, units),
+        functools.partial(kernel, nz, nb, lon, lat, ch, depth),
         out_shape=(
             jax.ShapeDtypeStruct(fields.shape, BF16),
             jax.ShapeDtypeStruct((9 * share, ch), F32),

time: 38.4 us -> 40 us (1.042)
  Pallas kernels: 37.6 us -> 39.1 us
    pallas_call x1, Pallas kernels: 35.8 us -> 37.3 us  [body(): pl.pallas_call(functools.partial(kernel, nz, nb, lon, lat, ch, depth), ou...]
where the time goes in v7:
time: 40 us; the launch traced here: 39.8 us
  Pallas kernels  39.1 us (98%)
  between operations  0.64 us (2%)
    pallas_call x1, Pallas kernels, body(): pl.pallas_call(functools.partial(kernel, nz, nb, lon, lat, ch, depth), ou...  37.3 us
    pallas_call x1, Pallas kernels, body(): pl.pallas_call(writer, out_shape=tuple((jax.ShapeDtypeStruct(r.shape, r.d...  1.8 us

profile of v7, /device:TPU:0, one launch (start us, length us, event | category | flops | bytes accessed | tf_op | source)
XLA Modules:
  0.0 39.8 jit_solution(6370284502135537396)
XLA Ops:
  0.6 37.3 %shard_map.110 = (bf16[1,8,64,128]{3,2,1,0:T(8,128)(2,1)}, f32[288,128]{1,0:T(8,128)}, f32[288,128]{1,0:T(8,128)}, f32[1,128]{1,0:T(1,128)}, f32[1,128]{1,0:T(1,128)}) custom-call(bf16[1,8,64,128]{3,2,1,0:T(8,128)(2,1)} %fields_h.1, s32[8,64]{1,0:T(8,128)} %land_h.1, bf16[3,384,128]{2,1,0:T(8,128)(2,1)} %bitcast.12, bf16[3,384,128]{2,1,0:T(8,128)(2,1)} %bitcast.13, ...), custom_call_target="tpu_custom_call" | custom-call | tf_op jit(solution)/shard_map/pallas_call | solution.py:622
  38.0 1.8 %shard_map.111 = (bf16[1,8,64,128]{3,2,1,0:T(8,128)(2,1)}, f32[288,128]{1,0:T(8,128)}, f32[288,128]{1,0:T(8,128)}, f32[1,128]{1,0:T(1,128)}, f32[1,128]{1,0:T(1,128)}) custom-call(bf16[1,8,64,128]{3,2,1,0:T(8,128)(2,1)} %get-tuple-element.15.refs_0_, f32[288,128]{1,0:T(8,128)} %get-tuple-element.16.refs_1_, f32[288,128]{1,0:T(8,128)} %get-tuple-element.17.refs_2_, ...), custom_call_target="tpu_custom_call" | custom-call | tf_op jit(solution)/shard_map/pallas_call | solution.py:643

commit v8 on v6

--- a/solution.py
+++ b/solution.py
@@ -502,15 +502,15 @@
         send_part(1, f, g, part_b, pair_b)
     loop(0, 3, tap_b)
 
+    after_pair(1, part_b, pair_b, half_b, cross_b)
+    after_cross(0, half_a, cross_a, mine_a, ring_a)
+    after_cross(1, half_b, cross_b, mine_b, ring_b)
+
     def finish_act(i):
         v = s_act[i + 1, :, ch:2 * ch].astype(F32)
         put(s_act, i + 1, shift_up(v, ghost_a[i + 1]), 2)
     loop(0, lon, finish_act)
-    after_pair(1, part_b, pair_b, half_b, cross_b)
-    conv_half(s_act, w_out, dact, 0)
-    after_cross(0, half_a, cross_a, mine_a, ring_a)
-    conv_half(s_act, w_out, dact, 1)
-    after_cross(1, half_b, cross_b, mine_b, ring_b)
+    conv(s_act, w_out, dact)
 
     def out_lon(i):
         output[0, i] = (dact[at(i)] * mask[at(i)]).astype(BF16)

time: 38.4 us -> 38.4 us (level)
  no operation moved by 1% of the time
where the time goes in v8:
time: 38.4 us; the launch traced here: 38.2 us
  Pallas kernels  37.6 us (98%)
  between operations  0.64 us (2%)
    pallas_call x1, Pallas kernels, body(): pl.pallas_call(functools.partial(kernel, nz, nb, lon, lat, ch, units), ou...  35.8 us
    pallas_call x1, Pallas kernels, body(): pl.pallas_call(writer, out_shape=tuple((jax.ShapeDtypeStruct(r.shape, r.d...  1.8 us

profile of v8, /device:TPU:0, one launch (start us, length us, event | category | flops | bytes accessed | tf_op | source)
XLA Modules:
  0.0 38.2 jit_solution(17778791954995233623)
XLA Ops:
  0.6 35.8 %shard_map.110 = (bf16[1,8,64,128]{3,2,1,0:T(8,128)(2,1)}, f32[288,128]{1,0:T(8,128)}, f32[288,128]{1,0:T(8,128)}, f32[1,128]{1,0:T(1,128)}, f32[1,128]{1,0:T(1,128)}) custom-call(bf16[1,8,64,128]{3,2,1,0:T(8,128)(2,1)} %fields_h.1, s32[8,64]{1,0:T(8,128)} %land_h.1, bf16[3,384,128]{2,1,0:T(8,128)(2,1)} %bitcast.12, bf16[3,384,128]{2,1,0:T(8,128)(2,1)} %bitcast.13, ...), custom_call_target="tpu_custom_call" | custom-call | tf_op jit(solution)/shard_map/pallas_call | solution.py:616
  36.4 1.8 %shard_map.111 = (bf16[1,8,64,128]{3,2,1,0:T(8,128)(2,1)}, f32[288,128]{1,0:T(8,128)}, f32[288,128]{1,0:T(8,128)}, f32[1,128]{1,0:T(1,128)}, f32[1,128]{1,0:T(1,128)}) custom-call(bf16[1,8,64,128]{3,2,1,0:T(8,128)(2,1)} %get-tuple-element.15.refs_0_, f32[288,128]{1,0:T(8,128)} %get-tuple-element.16.refs_1_, f32[288,128]{1,0:T(8,128)} %get-tuple-element.17.refs_2_, ...), custom_call_target="tpu_custom_call" | custom-call | tf_op jit(solution)/shard_map/pallas_call | solution.py:637
